TPU v7x, 256 devices: a whole 4x4x8 slice. The times are simulated.
256 devices in a mesh: engine: 32 (over x, z_hi, y), tensor: 8 (over z_lo, core).
Axes of the slice: x: 4, y: 4, z: 8 (z_hi: 2, z_lo: 4; z = z_hi * 4 + z_lo), core: 2. Of those that a mesh axis runs over, the one named last changes fastest.
Arguments:
- token_states: bfloat16 [512, 20, 5120], P('engine', None, 'tensor'), may hold values from -6 to 6
- row_len: int32 [512], P('engine'), may hold values from 1 to 20
- row_dest: int32 [512], P('engine'), may hold values from 0 to 31, as said below
- norm_gain: float32 [2, 5120], replicated, may hold values from 0.1 to 1.9
- q_gain: float32 [128], replicated, may hold values from 0.1 to 1.9
- k_gain: float32 [2, 128], replicated, may hold values from 0.1 to 1.9
- q_weight: bfloat16 [5120, 4096], P('engine', 'tensor'), may hold values from -0.078125 to 0.078125
- kv_weight0: bfloat16 [5120, 2, 1024], P('engine', None, 'tensor'), may hold values from -0.078125 to 0.078125
- out_weight: bfloat16 [5120, 4096], P('engine', 'tensor'), may hold values from -0.09375 to 0.09375
- kv_weight1: bfloat16 [5120, 2, 1024], P('engine', None, 'tensor'), may hold values from -0.078125 to 0.078125
Outputs:
- caches: bfloat16 [2, 2, 1024, 20, 1024], P(None, None, 'engine', None, 'tensor')
Inputs may be any that keep to these rules, and one draw needn't show every extreme that they name: `row_dest`: every engine receives 0, 16 or 32 rows: a quarter of the engines 2 * 16, a half 16. No engine sends more than 1 row to one engine.
All inputs are finite; a program needn't handle non-finite values.
Results may differ from a plain program's by a relative error of at most 0.012.
Values may be sent and summed in bfloat16 or wider, within the bound.
A program may use at most 128 MiB of HBM per device.

v0:
```python
import jax
import jax.numpy as jnp
from jax import lax
from jax.sharding import PartitionSpec as P

NORM_EPSILON = 1e-06
ROTARY_BASE = 1000000.0


def root_norm(values, gain_row):
    return (
        values
        * lax.rsqrt(jnp.mean(values * values, axis=-1, keepdims=True) + NORM_EPSILON)
        * gain_row
    )


def rotary(values, positions):
    half_dim = values.shape[-1] // 2
    frequency = jnp.power(
        ROTARY_BASE, -jnp.arange(half_dim, dtype=jnp.float32) * 2.0 / (2 * half_dim)
    )
    angles = positions.astype(jnp.float32)[:, None] * frequency[None, :]
    cosine = jnp.cos(angles)[:, None, :]
    sine_part = jnp.sin(angles)[:, None, :]
    lower_half = values[..., :half_dim]
    upper_half = values[..., half_dim:]
    return jnp.concatenate(
        [
            lower_half * cosine - upper_half * sine_part,
            upper_half * cosine + lower_half * sine_part,
        ],
        axis=-1,
    )


def attend(queries, keys_in, values_in):
    span = queries.shape[1]
    head_dim = queries.shape[-1]
    scores = jnp.einsum(
        "nikgd,njkd->nkgij", queries, keys_in, preferred_element_type=jnp.float32
    ) / jnp.sqrt(jnp.float32(head_dim))
    causal = jnp.arange(span)[:, None] >= jnp.arange(span)[None, :]
    weights = jnp.where(causal, jnp.exp(scores), jnp.float32(0.0))
    probabilities = (weights / jnp.sum(weights, axis=-1, keepdims=True)).astype(jnp.bfloat16)
    result = jnp.einsum(
        "nkgij,njkd->nikgd", probabilities, values_in, preferred_element_type=jnp.float32
    )
    return result.astype(jnp.bfloat16)


def prefill(states, norm_gain, q_gain, k_gain, q_weight, kv_weight0, out_weight, kv_weight1):
    row_count, row_span, _ = states.shape
    tokens = row_count * row_span
    head_dim = q_gain.shape[0]
    cache_width = kv_weight0.shape[2]
    cache_heads = cache_width // head_dim
    query_width = q_weight.shape[1]
    query_heads = query_width // head_dim
    group_size = query_heads // cache_heads
    positions = jnp.arange(row_span, dtype=jnp.int32)
    gathered = lax.all_gather(states, "tensor", axis=2, tiled=True)
    flat_rows = gathered.reshape(tokens, gathered.shape[2])
    normed0 = root_norm(flat_rows.astype(jnp.float32), norm_gain[0]).astype(jnp.bfloat16)
    columns = normed0
    queries = jnp.dot(
        columns,
        lax.all_gather(q_weight, "engine", axis=0, tiled=True),
        preferred_element_type=jnp.float32,
    )
    key_value = jnp.einsum(
        "td,dkc->tkc",
        columns,
        lax.all_gather(kv_weight0, "engine", axis=0, tiled=True),
        preferred_element_type=jnp.float32,
    )
    queries = rotary(
        root_norm(queries.reshape(row_count, row_span, query_heads, head_dim), q_gain), positions
    ).astype(jnp.bfloat16)
    key_value = key_value.reshape(row_count, row_span, 2, cache_heads, head_dim)
    first_keys = rotary(root_norm(key_value[:, :, 0], k_gain[0]), positions).astype(jnp.bfloat16)
    first_values = key_value[:, :, 1].astype(jnp.bfloat16)
    attended = attend(
        queries.reshape(row_count, row_span, cache_heads, group_size, head_dim),
        first_keys,
        first_values,
    )
    attended = attended.reshape(tokens, query_width)
    partial_value = lax.dot_general(
        attended,
        lax.all_gather(out_weight, "engine", axis=0, tiled=True),
        (((1,), (1,)), ((), ())),
        preferred_element_type=jnp.float32,
    )
    summed = lax.psum(partial_value.astype(jnp.bfloat16), "tensor").astype(jnp.float32)
    normed1 = root_norm(flat_rows.astype(jnp.float32) + summed, norm_gain[1]).astype(jnp.bfloat16)
    columns = normed1
    second_pair = jnp.einsum(
        "td,dkc->tkc",
        columns,
        lax.all_gather(kv_weight1, "engine", axis=0, tiled=True),
        preferred_element_type=jnp.float32,
    )
    second_pair = second_pair.reshape(row_count, row_span, 2, cache_heads, head_dim)
    second_keys = rotary(root_norm(second_pair[:, :, 0], k_gain[1]), positions).astype(jnp.bfloat16)
    second_values = second_pair[:, :, 1].astype(jnp.bfloat16)
    stacked = jnp.stack([first_keys, first_values, second_keys, second_values], axis=2)
    return stacked.reshape(row_count, row_span, 4, cache_width)


def body(
    token_states,
    row_len,
    row_dest,
    norm_gain,
    q_gain,
    k_gain,
    q_weight,
    kv_weight0,
    out_weight,
    kv_weight1,
):
    rows_here, row_span, _ = token_states.shape
    engines = lax.axis_size("engine")
    my_engine = lax.axis_index("engine")
    slot_count = 2 * rows_here
    all_dest, all_len = (
        lax.all_gather(row_dest, "engine", axis=0, tiled=True),
        lax.all_gather(row_len, "engine", axis=0, tiled=True),
    )
    send_pick = (jnp.arange(engines, dtype=jnp.int32)[:, None] == row_dest[None, :]).astype(
        jnp.bfloat16
    )
    to_me = (all_dest == my_engine).astype(jnp.int32)
    source = jnp.arange(engines * rows_here, dtype=jnp.int32) // rows_here
    slot_index = jnp.cumsum(to_me) - 1
    to_slot = (slot_index[None, :] == jnp.arange(slot_count, dtype=jnp.int32)[:, None]) & (
        to_me[None, :] == 1
    )
    lane_hit = source[:, None] == jnp.arange(engines, dtype=jnp.int32)[None, :]
    recv_pick = jnp.dot(
        to_slot.astype(jnp.bfloat16),
        lane_hit.astype(jnp.bfloat16),
        preferred_element_type=jnp.float32,
    ).astype(jnp.bfloat16)
    slot_len = jnp.sum(jnp.where(to_slot, all_len[None, :], 0), axis=1)
    outgoing = jnp.einsum(
        "pr,rlf->plf", send_pick, token_states, preferred_element_type=jnp.float32
    ).astype(jnp.bfloat16)
    arrived = lax.all_to_all(outgoing, "engine", split_axis=0, concat_axis=0, tiled=True)
    placed = jnp.einsum(
        "sp,plf->slf", recv_pick, arrived, preferred_element_type=jnp.float32
    ).astype(jnp.bfloat16)
    caches = prefill(
        placed, norm_gain, q_gain, k_gain, q_weight, kv_weight0, out_weight, kv_weight1
    )
    cache_width = caches.shape[3]
    live_mask = jnp.arange(row_span, dtype=jnp.int32)[None, :] < slot_len[:, None]
    caches = jnp.where(live_mask[:, :, None, None], caches, jnp.zeros((), jnp.bfloat16))
    return caches.reshape(slot_count, row_span, 2, 2, cache_width).transpose(2, 3, 0, 1, 4)


def solution(mesh):
    in_specs = (
        P("engine", None, "tensor"),
        P("engine"),
        P("engine"),
        P(),
        P(),
        P(),
        P("engine", "tensor"),
        P("engine", None, "tensor"),
        P("engine", "tensor"),
        P("engine", None, "tensor"),
    )
    out_specs = P(None, None, "engine", None, "tensor")
    return jax.shard_map(body, mesh=mesh, in_specs=in_specs, out_specs=out_specs, check_vma=False)
```

profile of v0, /device:TPU:39, one launch (start us, length us, event | category | flops | bytes accessed | tf_op | source)
XLA Modules:
  0.0 700.1 jit_solution(15747028382733773661)
XLA Ops:
  6.5 0.0 all-gather.8.cloned.1.call-start
  6.6 0.7 all-gather.8.cloned.1.call-update
  7.3 0.0 all-gather.10.cloned.1.call-start
  7.3 0.7 all-gather.10.cloned.1.call-update
  8.0 1.1 convolution_convert_fusion.2
  9.2 1.2 copy.56
  10.4 12.9 %all-to-all-start = ((bf16[32,20,640]{2,1,0:T(8,128)(2,1)}), bf16[32,20,640]{2,1,0:T(8,128)(2,1)S(1)}, u32[]{:S(2)}, u32[]{:S(2)}) async-start(bf16[32,20,640]{2,1,0:T(8,128)(2,1)} %copy.56), calls=%async_computation | async-start | bytes 1966080 | tf_op jit(solution)/shard_map/all_to_all | solution.py:150
  23.3 0.0 all-gather.6.cloned.1.call-start
  23.4 0.6 dynamic-slice
  24.7 0.2 dynamic-update-slice
  24.9 0.2 dynamic-update-slice.1
  25.1 29.6 %all-reduce.2 = (s32[512]{0:T(512)S(1)}, s32[512]{0:T(512)S(1)}) all-reduce(s32[512]{0:T(512)S(1)} %dynamic-update-slice, s32[512]{0:T(512)S(1)} %dynamic-update-slice.1), channel_id=1, replica_groups=mesh['engine'=32,'tensor'=8] {'engine'}, use_global_device_ids=true, to_apply=%add | all-reduce | flops 1024 | bytes 8192
  54.7 0.3 reduce-window.9
  55.0 0.1 slice.50
  55.2 0.1 slice_reduce_fusion
  55.3 0.1 add_bitcast_fusion
  55.3 1.5 convolution_convert_fusion.1
  56.9 0.0 all-gather.6.cloned.1.call-update
  56.9 0.0 all-gather.12.cloned.1.call-start
  56.9 0.5 all-gather.12.cloned.1.call-update
  57.5 0.2 all-reduce.5.cloned.1.call-start
  57.8 0.1 multiply_cosine_fusion
  57.9 53.3 %all-gather.8.cloned.1.call-done = bf16[5120,2,128]{2,1,0:T(2,128)(2,1)} async-done(((bf16[160,2,128]{2,1,0:T(2,128)(2,1)}), bf16[5120,2,128]{2,1,0:T(2,128)(2,1)}) %all-gather.8.cloned.1.call-update) | async-done | bytes 2621456 | tf_op jit(solution)/shard_map/all_gather | solution.py:74
  111.2 5.9 copy.58
  117.1 115.4 %all-gather.10.cloned.1.call-done = bf16[5120,512]{1,0:T(8,128)(2,1)} async-done(((bf16[160,512]{1,0:T(8,128)(2,1)}), bf16[5120,512]{1,0:T(8,128)(2,1)}) %all-gather.10.cloned.1.call-update) | async-done | bytes 5242896 | tf_op jit(solution)/shard_map/all_gather | solution.py:68
  232.5 8.0 %copy.61 = bf16[512,5120]{1,0:T(8,128)(2,1)} copy(bf16[512,5120]{0,1:T(8,128)(2,1)} %bitcast.101) | data formatting | bytes 10485760 | tf_op jit(solution)/shard_map/dot_general | solution.py:66
  240.5 65.0 %all-gather.6.cloned.1.call-done = bf16[32,20,5120]{2,0,1:T(8,128)(2,1)} async-done(((bf16[32,20,640]{2,0,1:T(8,128)(2,1)}), bf16[32,20,5120]{2,0,1:T(8,128)(2,1)}) %all-gather.6.cloned.1.call-update) | async-done | bytes 6553616 | tf_op jit(solution)/shard_map/all_gather | solution.py:62
  305.5 4.4 multiply_reduce_fusion.1
  309.9 0.4 copy-done.2
  310.2 2.0 fusion.10
  312.3 0.2 multiply_reduce_fusion.4
  312.5 0.2 multiply_multiply_fusion.2
  312.6 0.2 subtract_convert_fusion.2
  312.8 0.1 maximum_bitcast_fusion.1
  313.0 3.9 multiply_reduce_fusion.2
  316.9 0.4 multiply_multiply_fusion
  317.3 0.6 subtract_convert_fusion
  317.9 0.4 pad_maximum_fusion
  318.3 1.5 fusion.42
  319.8 0.4 fusion.9
  320.3 0.3 copy.66
  320.5 108.5 %all-gather.12.cloned.1.call-done = bf16[5120,512]{1,0:T(8,128)(2,1)} async-done(((bf16[160,512]{1,0:T(8,128)(2,1)}), bf16[5120,512]{1,0:T(8,128)(2,1)}) %all-gather.12.cloned.1.call-update) | async-done | bytes 5242896 | tf_op jit(solution)/shard_map/all_gather | solution.py:91
  429.0 8.0 %convolution_convert_fusion = bf16[640,5120]{1,0:T(8,128)(2,1)} fusion(bf16[5120,512]{1,0:T(8,128)(2,1)} %all-gather.12.cloned.1.call-done, bf16[80,8,4,128]{3,2,1,0:T(4,128)(2,1)S(1)} %bitcast.112), kind=kOutput, calls=%fused_computation.5 | convolution fusion | flops 3358720000 | bytes 12451840 | tf_op jit(solution)/shard_map/dot_general | solution.py:89
  437.0 0.0 all-reduce.5.cloned.1.call-update
  437.1 0.0 all-gather.14.cloned.1.call-start
  437.1 0.8 copy-done.4
  437.9 0.7 copy.67
  438.6 0.1 select_reduce_fusion
  438.7 1.0 slice.105
  439.7 12.3 %copy.60 = f32[32,20,5120]{2,1,0:T(8,128)} copy(bf16[32,20,5120]{2,0,1:T(8,128)(2,1)} %all-gather.6.cloned.1.call-done) | data formatting | bytes 19660800 | tf_op jit(solution)/shard_map/convert_element_type | solution.py:64
  452.0 12.4 %reshape.389 = f32[640,5120]{1,0:T(8,128)} reshape(f32[32,20,5120]{2,1,0:T(8,128)} %copy.60) | data formatting | bytes 26214400 | tf_op jit(solution)/shard_map/convert_element_type | solution.py:64
  464.5 0.1 maximum_bitcast_fusion
  464.6 121.2 %all-reduce.5.cloned.1.call-done = bf16[640,5120]{1,0:T(8,128)(2,1)} async-done(((bf16[640,5120]{1,0:T(8,128)(2,1)}), bf16[640,5120]{1,0:T(8,128)(2,1)}) %all-reduce.5.cloned.1.call-update) | async-done | bytes 6553616 | tf_op jit(solution)/shard_map/psum | solution.py:95
  585.8 8.4 %multiply_reduce_fusion = f32[640]{0:T(1024)S(1)} fusion(f32[640,5120]{1,0:T(8,128)} %reshape.389, bf16[640,5120]{1,0:T(8,128)(2,1)} %all-reduce.5.cloned.1.call-done), kind=kLoop, calls=%fused_computation.1 | loop fusion | flops 13106560 | bytes 19663360 | tf_op jit(solution)/shard_map/reduce_sum | solution.py:13
  594.1 87.7 %all-gather.14.cloned.1.call-done = bf16[5120,2,128]{2,0,1:T(8,128)(2,1)} async-done(((bf16[160,2,128]{2,0,1:T(8,128)(2,1)}), bf16[5120,2,128]{2,0,1:T(8,128)(2,1)}) %all-gather.14.cloned.1.call-update) | async-done | bytes 2621456 | tf_op jit(solution)/shard_map/all_gather | solution.py:101
  681.8 8.6 %fusion.2 = f32[640,2,128]{2,0,1:T(8,128)S(1)} fusion(bf16[5120,2,128]{2,0,1:T(8,128)(2,1)} %all-gather.14.cloned.1.call-done, f32[640,5120]{1,0:T(8,128)} %reshape.389, bf16[640,5120]{1,0:T(8,128)(2,1)} %all-reduce.5.cloned.1.call-done, f32[5120]{0:T(1024)S(1)} %bitcast.113, f32[640]{0:T(1024)S(1)} %add_rsqrt_fusion.4), kind=kOutput, calls=%fused_computation.8 | convolution fusion | flops 1694105600 | bytes 22960640 | tf_op jit(solution)/shard_map/td,dkc->tkc/dot_general | solution.py:98
  690.4 0.5 copy.68
  690.9 0.2 slice.72
  691.2 0.3 slice.75
  691.5 0.2 multiply_reduce_fusion.3
  691.7 0.2 multiply_multiply_fusion.1
  691.9 0.2 fusion.24
  692.1 0.1 pad_maximum_fusion.1
  692.2 1.0 fusion.21
  (46 shorter events, 0.3 us)
Async XLA Ops:
  6.5 1.5 copy-start
  6.5 16.9 %copy-start.10 = (u32[256]{0:T(256)S(1)}, u32[256]{0:T(256)}, u32[]{:S(2)}) copy-start(u32[256]{0:T(256)} %constant.64) | copy-start | bytes 3076
  6.5 18.1 %copy-start.7 = (s32[16]{0:T(128)S(1)}, s32[16]{0:T(128)}, u32[]{:S(2)}) copy-start(s32[16]{0:T(128)} %param.12) | copy-start | bytes 196
  6.5 18.4 %copy-start.9 = (s32[16]{0:T(128)S(1)}, s32[16]{0:T(128)}, u32[]{:S(2)}) copy-start(s32[16]{0:T(128)} %param.11) | copy-start | bytes 196
  6.5 104.7 %all-gather.8.cloned.1.call-start = ((), (), s32[]{:S(2)}) async-start(), calls=%async_computation.2 | async-start | bytes 2703360 | tf_op jit(solution)/shard_map/all_gather | solution.py:74
  7.3 225.2 %all-gather.10.cloned.1.call-start = ((), (), s32[]{:S(2)}) async-start(), calls=%async_computation.3 | async-start | bytes 5406720 | tf_op jit(solution)/shard_map/all_gather | solution.py:68
  10.4 47.3 %copy-start.6 = (f32[2,128]{1,0:T(2,128)S(1)}, f32[2,128]{1,0:T(2,128)}, u32[]{:S(2)}) copy-start(f32[2,128]{1,0:T(2,128)} %param.15) | copy-start | bytes 3076
  10.4 47.5 %copy-start.5 = (f32[2,5120]{1,0:T(2,128)S(1)}, f32[2,5120]{1,0:T(2,128)}, u32[]{:S(2)}) copy-start(f32[2,5120]{1,0:T(2,128)} %param.13) | copy-start | bytes 122884
  10.4 44.9 %all-to-all-start = ((bf16[32,20,640]{2,1,0:T(8,128)(2,1)}), bf16[32,20,640]{2,1,0:T(8,128)(2,1)S(1)}, u32[]{:S(2)}, u32[]{:S(2)}) async-start(bf16[32,20,640]{2,1,0:T(8,128)(2,1)} %copy.56), calls=%async_computation | async-start | bytes 1966080 | tf_op jit(solution)/shard_map/all_to_all | solution.py:150
  23.3 282.2 %all-gather.6.cloned.1.call-start = ((), (), s32[]{:S(2)}) async-start(), calls=%async_computation.1 | async-start | bytes 7372800 | tf_op jit(solution)/shard_map/all_gather | solution.py:62
  56.9 372.2 %all-gather.12.cloned.1.call-start = ((), (), s32[]{:S(2)}) async-start(), calls=%async_computation.4 | async-start | bytes 5406720 | tf_op jit(solution)/shard_map/all_gather | solution.py:91
  57.5 528.3 %all-reduce.5.cloned.1.call-start = ((), (), s32[]{:S(2)}) async-start(), calls=%async_computation.5 | async-start | bytes 13107200 | tf_op jit(solution)/shard_map/psum | solution.py:95
  305.5 4.7 copy-start.2
  305.5 7.4 %slice-start = ((s8[5242880]{0:T(1024)(128)(4,1)}), s8[4194304]{0:T(1024)(128)(4,1)S(1)}, s32[]{:S(2)}) async-start(s8[5242880]{0:T(1024)(128)(4,1)} %bitcast.102), calls=%async_computation.7 | async-start | bytes 8388608
  310.2 2.7 slice-start.1
  312.3 6.0 copy-start.3
  313.0 3.9 copy-start.8
  437.0 0.9 copy-start.4
  437.1 244.7 %all-gather.14.cloned.1.call-start = ((), (), s32[]{:S(2)}) async-start(), calls=%async_computation.6 | async-start | bytes 2703360 | tf_op jit(solution)/shard_map/all_gather | solution.py:101
  691.2 2.0 copy-start.1
Sparse Core Ops, SparseCore 0:
  10.9 100.3 all-gather.7
  114.6 117.8 all-gather.9
  234.3 71.1 all-gather.5
  308.8 120.2 all-gather.11
  437.2 148.5 all-reduce.4
  589.1 92.7 all-gather.13
where the time goes:
time: 705 us; the launch traced here: 700 us
  waiting for transfers between devices  553 us (78%)
  local copies, waits for them, and re-layouts  45.4 us (6%)
  blocking collectives  29.6 us (4%)
  matrix products  27.1 us (4%)
  other arithmetic  17.2 us (2%)
  between operations  14.5 us (2%)
  starting transfers between devices  13.3 us (2%)
    psum x1, waiting for transfers between devices, prefill(): lax.psum(partial_value.astype(jnp.bfloat16), 'tensor').astype(jnp.float32)  121 us
    all_gather x1, waiting for transfers between devices, prefill(): lax.all_gather(q_weight, 'engine', axis=0, tiled=True)  115 us
    all_gather x1, waiting for transfers between devices, prefill(): lax.all_gather(out_weight, 'engine', axis=0, tiled=True)  109 us
    all_gather x1, waiting for transfers between devices, prefill(): lax.all_gather(kv_weight1, 'engine', axis=0, tiled=True)  87.7 us
    all_gather x1, waiting for transfers between devices, prefill(): gathered = lax.all_gather(states, 'tensor', axis=2, tiled=True)  65 us
    all_gather x1, waiting for transfers between devices, prefill(): lax.all_gather(kv_weight0, 'engine', axis=0, tiled=True)  53.3 us
    unnamed x1, blocking collectives  29.6 us
    convert_element_type x2, local copies, waits for them, and re-layouts, prefill(): flat_rows.astype(jnp.float32)  24.7 us
  transfers between devices with their start and end apart: 7, of which 6 were waited for; matrix products, arithmetic and copies ran while one was open for 10% of the time, Pallas kernels for 0%

commit v1 on v0

v1 whole, which is shorter than its diff:
```python
import functools

import jax
import jax.numpy as jnp
import numpy as np
from jax import lax
from jax.experimental import pallas as pl
from jax.experimental.pallas import tpu as pltpu
from jax.sharding import PartitionSpec as P

EPS = 1e-06
ROTARY_BASE = 1000000.0
MESH = pl.DeviceIdType.MESH
TOK = 320
SPAN = 20
WC = 768
CB = 80
F32 = jnp.float32
BF = jnp.bfloat16
NT = (((1,), (1,)), ((), ()))


def mod4(v):
    return lax.rem(v + 8, 4)


def device(x, y, z, c):
    z = lax.rem(z + 16, 8)
    return (mod4(x) * 8 + (z // 4) * 4 + mod4(y), lax.rem(z, 4) * 2 + c)


def rcopy(src, dst, send_sem, recv_sem, target):
    return pltpu.make_async_remote_copy(
        src_ref=src, dst_ref=dst, send_sem=send_sem, recv_sem=recv_sem,
        device_id=target, device_id_type=MESH,
    )


def rope(v, cos, sin):
    return v * cos + pltpu.roll(v, 64, 1) * sin


def head_norm(v, gain):
    return v * lax.rsqrt(jnp.mean(v * v, axis=1, keepdims=True) + EPS) * gain


class Gather:
    def __init__(self, buf, slot, me, ssem, rsem):
        self.buf, self.slot, self.me = buf, slot, me
        self.ssem, self.rsem = ssem, rsem
        self.sent = []

    def place(self, h, i, j, core=None):
        x, y, z, c = self.me
        c = c if core is None else core
        if h == 0:
            return self.slot(mod4(x + i), mod4(y + j), c)
        return self.slot(mod4(x + j), mod4(y + i), c)

    def to(self, h, axis, step):
        x, y, z, c = self.me
        if (h == 0) == (axis == 0):
            return device(x + step, y, z, c)
        return device(x, y + step, z, c)

    def view(self, slot, h, cols):
        return self.buf.at[slot, pl.ds(80 * h, 80), cols]

    def send(self, h, i, j, cols, target, k):
        ref = self.view(self.place(h, i, j), h, cols)
        cp = rcopy(ref, ref, self.ssem.at[h, k], self.rsem.at[h, k], target)
        cp.start()
        self.sent.append(cp)

    def recv(self, h, i, j, cols, k, core=None):
        ref = self.view(self.place(h, i, j, core), h, cols)
        rcopy(ref, ref, self.ssem.at[h, k], self.rsem.at[h, k], self.to(h, 0, 1)).wait_recv()

    ALL = slice(0, WC)
    LEFT = slice(0, WC // 2)
    RIGHT = slice(WC // 2, WC)
    OFF = (0, -1, 1, 2)

    def sibling(self, h, ii, jj):
        x, y, z, c = self.me
        self.send(h, self.OFF[ii], self.OFF[jj], self.ALL, device(x, y, z, 1 - c), 20 + 4 * ii + jj)

    def first(self):
        for h in range(2):
            self.send(h, 0, 0, self.ALL, self.to(h, 0, 1), 0)
            self.send(h, 0, 0, self.ALL, self.to(h, 0, -1), 1)
        for h in range(2):
            self.second_send(h, 0)
            self.sibling(h, 0, 0)

    def first_recv(self):
        for h in range(2):
            self.recv(h, -1, 0, self.ALL, 0)
            self.send(h, -1, 0, self.LEFT, self.to(h, 0, 1), 2)
            self.recv(h, 1, 0, self.ALL, 1)
            self.send(h, 1, 0, self.RIGHT, self.to(h, 0, -1), 3)
        for h in range(2):
            self.second_send(h, 1)
            self.second_send(h, 2)
            self.sibling(h, 1, 0)
            self.sibling(h, 2, 0)

    def first_last(self):
        for h in range(2):
            self.recv(h, 2, 0, self.LEFT, 2)
            self.recv(h, 2, 0, self.RIGHT, 3)
            self.second_send(h, 3)
            self.sibling(h, 3, 0)

    def second_send(self, h, ii):
        i = self.OFF[ii]
        self.send(h, i, 0, self.ALL, self.to(h, 1, 1), 4 + 2 * ii)
        self.send(h, i, 0, self.ALL, self.to(h, 1, -1), 5 + 2 * ii)

    def second_recv(self, ii):
        i = self.OFF[ii]
        for h in range(2):
            self.recv(h, i, -1, self.ALL, 4 + 2 * ii)
            self.send(h, i, -1, self.LEFT, self.to(h, 1, 1), 12 + 2 * ii)
            self.recv(h, i, 1, self.ALL, 5 + 2 * ii)
            self.send(h, i, 1, self.RIGHT, self.to(h, 1, -1), 13 + 2 * ii)
            self.sibling(h, ii, 1)
            self.sibling(h, ii, 2)

    def second_last(self, ii):
        i = self.OFF[ii]
        for h in range(2):
            self.recv(h, i, 2, self.LEFT, 12 + 2 * ii)
            self.recv(h, i, 2, self.RIGHT, 13 + 2 * ii)
            self.sibling(h, ii, 3)

    def finish(self):
        c = self.me[3]
        for h in range(2):
            for ii in range(4):
                for jj in range(4):
                    self.recv(h, self.OFF[ii], self.OFF[jj], self.ALL, 20 + 4 * ii + jj, 1 - c)

    def drain(self):
        for cp in self.sent:
            cp.wait_send()
        self.sent = []


class Ring:
    def __init__(self, buf, slot, me, ssem, rsem, cols):
        self.buf, self.slot, self.me = buf, slot, me
        self.ssem, self.rsem = ssem, rsem
        self.cols = cols
        self.sent = []

    def view(self, origin, half):
        return self.buf.at[self.slot(lax.rem(origin + 16, 8)), pl.ds(160 * half, 160)]

    def send(self, way, half, k, src=None):
        x, y, z, c = self.me
        d = 0 if way > 0 else 1
        ref = self.view(z - way * (k - 1), half)
        cp = rcopy(ref if src is None else src, ref, self.ssem.at[d, half, k - 1],
                   self.rsem.at[d, half, k - 1], device(x, y, z + way, c))
        cp.start()
        self.sent.append(cp)

    def recv(self, way, half, k):
        x, y, z, c = self.me
        d = 0 if way > 0 else 1
        ref = self.view(z - way * k, half)
        rcopy(ref, ref, self.ssem.at[d, half, k - 1], self.rsem.at[d, half, k - 1],
              device(x, y, z + way, c)).wait_recv()
        if k < 3 or (k == 3 and (half == 0) == (way > 0)):
            self.send(way, half, k + 1)

    def drain(self):
        for cp in self.sent:
            cp.wait_send()
        self.sent = []


def mega(x_in, wq_in, wo_in, info_in, g0, g1, qg, kg, cos, sin, mask, lanes,
         land, info_land,
         XX, WQ, WO, A, ACC, HID, HB, PP, RSS, RSR, SS, SEND, VAL, INFO,
         own_sem, swap_s, swap_r, xs, xr, xcs, xcr, wqs, wqr, ts, tr, wos, wor,
         as_, ar, rss, rsr, sss, ssr, es, er, ns, nr):
    e = lax.axis_index("engine")
    t = lax.axis_index("tensor")
    x, y, a = e // 8, lax.rem(e, 4), lax.rem(e // 4, 2)
    zl, c = t // 2, lax.rem(t, 2)
    z = a * 4 + zl
    me = (x, y, z, c)
    sib = device(x, y, z, 1 - c)
    partner = device(x, y, z + 4, 1 - c)
    moved = a != c
    t_to = device(x, 2 * y + 1 + zl, a * 4 + y, c)
    t_from = device(x, zl, a * 4 + mod4(y - 2 * zl - 1), c)

    bar = pltpu.get_barrier_semaphore()
    for other in (device(x + 1, y, z, c), device(x - 1, y, z, c), device(x, y + 1, z, c),
                  device(x, y - 1, z, c), device(x, y, z + 1, c), device(x, y, z - 1, c),
                  sib, partner, t_to, t_from):
        pl.semaphore_signal(bar, inc=1, device_id=other, device_id_type=MESH)
    pl.semaphore_wait(bar, 10)

    def x_slot(origin):
        oa, ol = origin // 4, lax.rem(origin, 4)
        return jnp.where(oa == c, 2 * ol + c, 8 + ol)

    def wq_slot(sx, sy, sc):
        return sx * 8 + sc * 4 + sy

    def wo_slot(sx, sy, sc):
        return (2 * mod4(sy - 2 * zl - 1) + sc) * 4 + sx

    swap_slot = x * 8 + a * 4 + y

    def swap_copies():
        return (
            rcopy(wq_in, WQ.at[swap_slot], swap_s.at[0], swap_r.at[0], partner),
            rcopy(info_in, INFO, swap_s.at[1], swap_r.at[1], partner),
        )

    def stay_copies():
        return (
            pltpu.make_async_copy(wq_in, WQ.at[swap_slot], own_sem.at[0]),
            pltpu.make_async_copy(info_in, INFO, own_sem.at[1]),
        )

    @pl.when(moved)
    def _():
        for cp in swap_copies():
            cp.start()

    @pl.when(jnp.logical_not(moved))
    def _():
        for cp in stay_copies():
            cp.start()

    ring = Ring(XX, x_slot, me, xs, xr, 640)
    for way, half in ((1, 0), (-1, 1), (1, 1), (-1, 0)):
        ring.send(way, half, 1, x_in.at[pl.ds(160 * half, 160)])
    own_x = pltpu.make_async_copy(x_in, XX.at[x_slot(z)], own_sem.at[2])
    own_x.start()

    def x_cross(origin, half, src=None):
        origin = lax.rem(origin + 16, 8)
        oa, ol = origin // 4, lax.rem(origin, 4)

        @pl.when(oa != c)
        def _():
            rows = pl.ds(160 * half, 160)
            rcopy(XX.at[8 + ol, rows] if src is None else src, XX.at[2 * ol + c, rows],
                  xcs.at[ol, half], xcr.at[ol, half], sib).start()

    def x_recv(way, half, k):
        ring.recv(way, half, k)
        x_cross(z - way * k, half)

    for half in range(2):
        x_cross(z, half, x_in.at[pl.ds(160 * half, 160)])

    x_recv(1, 0, 1)
    x_recv(-1, 1, 1)

    @pl.when(moved)
    def _():
        for cp in swap_copies():
            cp.wait()

    @pl.when(jnp.logical_not(moved))
    def _():
        for cp in stay_copies():
            cp.wait()

    gq = Gather(WQ, wq_slot, me, wqs, wqr)
    gq.first()
    x_recv(1, 1, 1)
    x_recv(-1, 0, 1)
    gq.first_recv()
    x_recv(1, 0, 2)
    x_recv(-1, 1, 2)
    gq.first_last()
    gq.second_recv(0)
    x_recv(1, 1, 2)
    x_recv(-1, 0, 2)
    gq.second_recv(1)
    gq.second_recv(2)
    gq.second_last(0)
    x_recv(1, 0, 3)
    x_recv(-1, 1, 3)
    t_slot = (2 * zl + c) * 4 + x
    shift = rcopy(wo_in, WO.at[t_slot], ts, tr, t_to)
    shift.start()
    gq.second_recv(3)
    gq.second_last(1)
    x_recv(1, 1, 3)
    x_recv(-1, 0, 3)
    gq.second_last(2)
    gq.second_last(3)
    x_recv(1, 0, 4)
    x_recv(-1, 1, 4)
    shift.wait_send()
    t_mine = wo_slot(x, y, c)
    rcopy(wo_in, WO.at[t_mine], ts, tr, t_to).wait_recv()
    go = Gather(WO, wo_slot, me, wos, wor)
    go.first()
    gq.finish()
    own_x.wait()
    for ol in range(4):
        for half in range(2):
            rows = pl.ds(160 * half, 160)
            rcopy(XX.at[8 + ol, rows], XX.at[2 * ol + 1 - c, rows],
                  xcs.at[ol, half], xcr.at[ol, half], sib).wait_recv()

    ACC[...] = jnp.zeros_like(ACC)

    def qkv_step(i, total):
        xv = XX[i].astype(F32)
        total = total + jnp.sum(xv * xv, axis=1, keepdims=True)
        xn = (xv * g0[i]).astype(BF)
        w = WQ[pl.ds(4 * i, 4)].reshape(640, WC)
        ACC[...] += jnp.dot(xn, w, preferred_element_type=F32)
        return total

    total = lax.fori_loop(0, 8, qkv_step, jnp.zeros((TOK, 1), F32))
    r0 = lax.rsqrt(total / 5120.0 + EPS)
    go.first_recv()
    cosv, sinv = cos[...], sin[...]
    VAL[:, 0:128] = rope(head_norm(ACC[:, 512:640] * r0, kg[0:1]), cosv, sinv).astype(BF)
    VAL[:, 128:256] = (ACC[:, 640:768] * r0).astype(BF)
    for g in range(4):
        cols = slice(128 * g, 128 * g + 128)
        A[z, :, cols] = rope(head_norm(ACC[:, cols] * r0, qg[...]), cosv, sinv).astype(BF)
    go.first_last()
    for n in range(TOK // CB):
        rows = slice(CB * n, CB * n + CB)
        q = jnp.concatenate([A[z, rows, 128 * g:128 * g + 128] for g in range(4)], axis=0)
        s = lax.dot_general(q, VAL[rows, 0:128], NT, preferred_element_type=F32)
        w = jnp.where(mask[...] > 0, jnp.exp(s / jnp.sqrt(F32(128.0))), 0.0)
        p = (w / jnp.sum(w, axis=1, keepdims=True)).astype(BF)
        o = jnp.dot(p, VAL[rows, 128:256], preferred_element_type=F32).astype(BF)
        for g in range(4):
            A[z, rows, 128 * g:128 * g + 128] = o[CB * g:CB * g + CB]

    att = Ring(A, lambda origin: origin, me, as_, ar, 512)
    for way, half in ((1, 0), (-1, 1), (1, 1), (-1, 0)):
        att.send(way, half, 1)
    go.second_recv(0)

    def exchange_target(d):
        return (d, 2 * zl + a)

    mine = x * 8 + c * 4 + y

    def same(d):
        return jnp.logical_and(d == e, a == c)

    def list_step(d, carry):
        @pl.when(same(d))
        def _():
            pltpu.make_async_copy(INFO, info_land.at[mine], nr.at[mine]).start()

        @pl.when(jnp.logical_not(same(d)))
        def _():
            rcopy(INFO, info_land.at[mine], ns.at[d], nr.at[mine], exchange_target(d)).start()
        return carry

    pick_row = lax.broadcasted_iota(jnp.int32, (640, 160), 0)
    pick_col = lax.broadcasted_iota(jnp.int32, (640, 160), 1)
    pick = (pick_row == pick_col + 160 * zl).astype(BF)
    for sx in range(4):
        HID[sx] = jnp.dot(XX[2 * sx + a], pick, preferred_element_type=F32)

    def out_step(origin):
        origin = lax.rem(origin + 16, 8)
        head = 2 * lax.rem(origin, 4) + origin // 4

        def one(sx, carry):
            w = WO[head * 4 + sx, :, 0:512]
            part = lax.dot_general(A[origin], w, NT, preferred_element_type=F32)
            HID[sx] += part.astype(BF).astype(F32)
            return carry

        lax.fori_loop(0, 4, one, 0)

    att.recv(1, 0, 1)
    att.recv(-1, 1, 1)
    go.second_recv(1)
    att.recv(1, 1, 1)
    att.recv(-1, 0, 1)
    go.second_recv(2)
    go.second_last(0)
    att.recv(1, 0, 2)
    att.recv(-1, 1, 2)
    go.second_recv(3)
    go.second_last(1)
    att.recv(1, 1, 2)
    att.recv(-1, 0, 2)
    go.second_last(2)
    go.second_last(3)
    go.finish()
    out_step(z)
    out_step(z - 1)
    out_step(z + 1)
    att.recv(1, 0, 3)
    att.recv(-1, 1, 3)
    out_step(z - 2)
    out_step(z + 2)
    att.recv(1, 1, 3)
    att.recv(-1, 0, 3)
    lax.fori_loop(0, 32, list_step, 0)
    out_step(z - 3)
    out_step(z + 3)
    att.recv(1, 0, 4)
    att.recv(-1, 1, 4)
    out_step(z + 4)

    col = jnp.zeros((TOK, 1), F32)
    for sx in range(4):
        hv = HID[sx]
        col = col + jnp.sum(hv * hv, axis=1, keepdims=True)
        HB[sx] = (hv * g1[sx * 8 + a * 4 + zl]).astype(BF)
    eye = (lax.broadcasted_iota(jnp.int32, (TOK, TOK), 0)
           == lax.broadcasted_iota(jnp.int32, (TOK, TOK), 1))
    SS[z] = jnp.sum(jnp.where(eye, col, 0.0), axis=0, keepdims=True)
    ss_sent = []
    for k in range(1, 8):
        cp = rcopy(SS.at[z], SS.at[z], sss.at[k], ssr.at[k], device(x, y, z + k, c))
        cp.start()
        ss_sent.append(cp)

    def partial(dest):
        dest = lax.rem(dest + 16, 8)
        head = 2 * lax.rem(dest, 4) + dest // 4
        out = jnp.dot(HB[0], WO[head * 4, :, 512:768], preferred_element_type=F32)
        for sx in range(1, 4):
            out = out + jnp.dot(HB[sx], WO[head * 4 + sx, :, 512:768], preferred_element_type=F32)
        PP[dest] = out

    rs_sent = []

    def rs_send(way, half, s, value):
        d = 0 if way > 0 else 1
        RSS[d, half, s] = value.astype(BF)
        cp = rcopy(RSS.at[d, half, s], RSR.at[d, half, s], rss.at[d, half, s],
                   rsr.at[d, half, s], device(x, y, z + way, c))
        cp.start()
        rs_sent.append(cp)

    def rs_recv(way, half, s):
        d = 0 if way > 0 else 1
        rcopy(RSS.at[d, half, s], RSR.at[d, half, s], rss.at[d, half, s],
              rsr.at[d, half, s], device(x, y, z + way, c)).wait_recv()
        return RSR[d, half, s].astype(F32)

    def hops(way, half):
        return 4 if (half == 0) == (way > 0) else 3

    def own_part(way, half, s):
        dest = lax.rem(z + way * (hops(way, half) - s) + 16, 8)
        return PP[dest, pl.ds(160 * half, 160)]

    order = ((1, 0), (-1, 1), (1, 1), (-1, 0))
    partial(z + 4)
    rs_send(1, 0, 0, own_part(1, 0, 0))
    rs_send(-1, 1, 0, own_part(-1, 1, 0))
    partial(z + 3)
    rs_send(1, 1, 0, own_part(1, 1, 0))
    partial(z - 3)
    rs_send(-1, 0, 0, own_part(-1, 0, 0))
    partial(z + 2)
    partial(z - 2)
    partial(z + 1)
    partial(z - 1)
    partial(z)
    for s in range(3):
        for way, half in order:
            last = hops(way, half) - 1
            if s < last:
                rs_send(way, half, s + 1, rs_recv(way, half, s) + own_part(way, half, s + 1))
    ss_total = SS[z]
    for k in range(1, 8):
        origin = lax.rem(z - k + 16, 8)
        rcopy(SS.at[origin], SS.at[origin], sss.at[k], ssr.at[k], device(x, y, z + k, c)).wait_recv()
        ss_total = ss_total + SS[origin]
    r1 = lax.rsqrt(jnp.sum(jnp.where(eye, ss_total, 0.0), axis=1, keepdims=True) / 5120.0 + EPS)

    info = jnp.broadcast_to(INFO[...].astype(F32), (8, 128)).astype(BF)
    er_ = lax.broadcasted_iota(jnp.int32, (128, TOK), 0)
    row_of, tok_of = lanes[0:1, :], lanes[1:2, :]
    dest_l = jnp.dot(info, (er_ == row_of).astype(BF), preferred_element_type=F32)[0:1]
    len_l = jnp.dot(info, (er_ == row_of + 16).astype(BF), preferred_element_type=F32)[0:1]
    dest_l = dest_l.astype(jnp.int32)
    live = tok_of < len_l.astype(jnp.int32)
    key_a = jnp.where(jnp.logical_and(live, tok_of < 16), dest_l * 16 + tok_of, -1000)
    key_b = jnp.where(jnp.logical_and(live, tok_of >= 16), dest_l * 16 + tok_of - 16, -1000)
    place = lax.broadcasted_iota(jnp.int32, (512, TOK), 0)

    for half in range(2):
        way = 1 if half == 0 else -1
        rows = slice(160 * half, 160 * half + 160)
        kv = PP[z, rows] + rs_recv(way, half, 3) + rs_recv(-way, half, 2)
        kv = kv * r1[rows]
        VAL[rows, 256:384] = rope(head_norm(kv[:, 0:128], kg[1:2]), cos[rows], sin[rows]).astype(BF)
        VAL[rows, 384:512] = kv[:, 128:256].astype(BF)

    head_rows = jnp.dot((place == key_a).astype(BF), VAL[...], preferred_element_type=F32).astype(BF)
    SEND[:, :, 0:512] = head_rows.reshape(32, 16, 512)
    tail = jnp.zeros((512, 128), F32)
    for f in range(4):
        tail = tail + jnp.dot((place == key_b + 4 * f).astype(BF), VAL[:, 128 * f:128 * f + 128],
                              preferred_element_type=F32)
    SEND[:, :, 512:640] = tail.astype(BF).reshape(32, 16, 128)

    def send_step(d, carry):
        @pl.when(same(d))
        def _():
            pltpu.make_async_copy(SEND.at[d], land.at[mine], er.at[mine]).start()

        @pl.when(jnp.logical_not(same(d)))
        def _():
            rcopy(SEND.at[d], land.at[mine], es.at[d], er.at[mine], exchange_target(d)).start()
        return carry

    lax.fori_loop(0, 32, send_step, 0)

    def recv_step(s, carry):
        rcopy(SEND.at[s], land.at[s], es.at[s], er.at[s], exchange_target(s)).wait_recv()
        rcopy(INFO, info_land.at[s], ns.at[s], nr.at[s], exchange_target(s)).wait_recv()

        @pl.when(jnp.logical_not(same(s)))
        def _():
            rcopy(SEND.at[s], land.at[s], es.at[s], er.at[s], exchange_target(s)).wait_send()
            rcopy(INFO, info_land.at[s], ns.at[s], nr.at[s], exchange_target(s)).wait_send()
        return carry

    lax.fori_loop(0, 32, recv_step, 0)

    for part in (ring, gq, go, att):
        part.drain()
    for cp in ss_sent + rs_sent:
        cp.wait_send()
    for ol in range(4):
        @pl.when(c == 0)
        def _(ol=ol):
            for half in range(2):
                rows = pl.ds(160 * half, 160)
                rcopy(XX.at[8 + ol, rows], XX.at[2 * ol, rows], xcs.at[ol, half], xcr.at[ol, half], sib).wait_send()

        @pl.when(c == 1)
        def _(ol=ol):
            for half in range(2):
                rows = pl.ds(160 * half, 160)
                rcopy(XX.at[8 + ol, rows], XX.at[2 * ol + 1, rows], xcs.at[ol, half], xcr.at[ol, half], sib).wait_send()


def place_rows(land, key, out):
    at = lax.broadcasted_iota(jnp.int32, (512, 512), 0)
    pick = (at == key[...]).astype(BF)
    rows = jnp.dot(pick, land[...].reshape(512, 640), preferred_element_type=F32).astype(BF)
    rows = rows.reshape(32, 16, 640)
    for f in range(4):
        out[f, :, 0:16, :] = rows[:, :, 128 * f:128 * f + 128]
        out[f, :, 16:20, :] = rows[:, 4 * f:4 * f + 4, 512:640]


def tables():
    half = 64
    pos = (np.arange(TOK) % SPAN).astype(np.float32)
    freq = np.power(ROTARY_BASE, -np.arange(half, dtype=np.float64) * 2.0 / 128).astype(np.float32)
    angle = (pos[:, None] * freq[None, :]).astype(np.float32).astype(np.float64)
    cos, sin = np.cos(angle), np.sin(angle)
    cos = np.concatenate([cos, cos], axis=1).astype(np.float32)
    sin = np.concatenate([-sin, sin], axis=1).astype(np.float32)
    i, j = np.arange(CB)[:, None], np.arange(CB)[None, :]
    mask = ((i // SPAN == j // SPAN) & (j <= i)).astype(np.float32)
    mask = np.tile(mask, (4, 1))
    lanes = np.zeros((8, TOK), np.int32)
    lanes[0] = np.arange(TOK) // SPAN
    lanes[1] = np.arange(TOK) % SPAN
    return cos, sin, mask, lanes


def body(token_states, row_len, row_dest, norm_gain, q_gain, k_gain,
         q_weight, kv_weight0, out_weight, kv_weight1):
    x2 = token_states.reshape(TOK, 640)
    wq = jnp.concatenate([q_weight, kv_weight0.reshape(160, 256)], axis=1)
    wo = jnp.concatenate([out_weight, kv_weight1.reshape(160, 256)], axis=1)
    info = jnp.concatenate([row_dest, row_len, jnp.zeros((96,), jnp.int32)]).reshape(1, 128)
    g0 = norm_gain[0].reshape(8, 1, 640)
    g1 = norm_gain[1].reshape(32, 1, 160)
    cos, sin, mask, lanes = tables()
    vm = pl.BlockSpec(memory_space=pltpu.VMEM)
    hbm = pl.BlockSpec(memory_space=pl.ANY)
    dma = pltpu.SemaphoreType.DMA
    land, info_land = pl.pallas_call(
        mega,
        out_shape=(jax.ShapeDtypeStruct((32, 16, 640), BF),
                   jax.ShapeDtypeStruct((32, 1, 128), jnp.int32)),
        in_specs=[hbm, hbm, hbm, hbm] + [vm] * 8,
        out_specs=(vm, vm),
        scratch_shapes=[
            pltpu.VMEM((12, TOK, 640), BF),
            pltpu.VMEM((32, 160, WC), BF),
            pltpu.VMEM((32, 160, WC), BF),
            pltpu.VMEM((8, TOK, 512), BF),
            pltpu.VMEM((TOK, WC), F32),
            pltpu.VMEM((4, TOK, 160), F32),
            pltpu.VMEM((4, TOK, 160), BF),
            pltpu.VMEM((8, TOK, 256), F32),
            pltpu.VMEM((2, 2, 4, 160, 256), BF),
            pltpu.VMEM((2, 2, 4, 160, 256), BF),
            pltpu.VMEM((8, 1, TOK), F32),
            pltpu.VMEM((32, 16, 640), BF),
            pltpu.VMEM((TOK, 512), BF),
            pltpu.VMEM((1, 128), jnp.int32),
            dma((3,)), dma((2,)), dma((2,)),
            dma((2, 2, 4)), dma((2, 2, 4)), dma((4, 2)), dma((4, 2)),
            dma((2, 36)), dma((2, 36)), dma, dma, dma((2, 36)), dma((2, 36)),
            dma((2, 2, 4)), dma((2, 2, 4)), dma((2, 2, 4)), dma((2, 2, 4)),
            dma((8,)), dma((8,)), dma((32,)), dma((32,)), dma((32,)), dma((32,)),
        ],
        compiler_params=pltpu.CompilerParams(
            collective_id=0, has_side_effects=True, vmem_limit_bytes=56 * 2**20),
        name="prefill",
    )(x2, wq, wo, info, g0, g1, q_gain.reshape(1, 128), k_gain,
      jnp.asarray(cos), jnp.asarray(sin), jnp.asarray(mask), jnp.asarray(lanes))
    mine = lax.axis_index("engine")
    here = jnp.any(info_land[:, 0, :16] == mine, axis=1)
    slot = jnp.cumsum(here.astype(jnp.int32)) - 1
    key = jnp.where(here, slot * 16, -1000)[:, None] + jnp.arange(16, dtype=jnp.int32)[None, :]
    out = pl.pallas_call(
        place_rows,
        out_shape=jax.ShapeDtypeStruct((4, 32, SPAN, 128), BF),
        in_specs=[vm, vm],
        out_specs=vm,
        compiler_params=pltpu.CompilerParams(vmem_limit_bytes=32 * 2**20),
        name="place_rows",
    )(land, key.reshape(1, 512))
    return out.reshape(2, 2, 32, SPAN, 128)


def solution(mesh):
    in_specs = (
        P("engine", None, "tensor"), P("engine"), P("engine"), P(), P(), P(),
        P("engine", "tensor"), P("engine", None, "tensor"),
        P("engine", "tensor"), P("engine", None, "tensor"),
    )
    out_specs = P(None, None, "engine", None, "tensor")
    return jax.shard_map(body, mesh=mesh, in_specs=in_specs, out_specs=out_specs, check_vma=False)
```

time: 705 us -> 155 us (0.22)
  waiting for transfers between devices: 553 us -> 0 us
  Pallas kernels: 0 us -> 145 us
  local copies, waits for them, and re-layouts: 45.4 us -> 7 us
  blocking collectives: 29.6 us -> 0 us
  matrix products: 27.1 us -> 0 us
  between operations: 14.5 us -> 0.09 us
  other arithmetic: 17.2 us -> 3.06 us
  starting transfers between devices: 13.3 us -> 0 us
    all_gather x5 -> x0, waiting for transfers between devices: 430 us -> none  [the longest x1 115 us: prefill(): lax.all_gather(q_weight, 'engine', axis=0, tiled=True)]
    pallas_call x0 -> x2, Pallas kernels: none -> 145 us  [the longest x1 144 us: body(): pl.pallas_call(mega, out_shape=(jax.ShapeDtypeStruct((32, 16, 640), BF),...]
    psum x1 -> x0, waiting for transfers between devices: 121 us -> none  [prefill(): lax.psum(partial_value.astype(jnp.bfloat16), 'tensor').astype(jnp.float32)]
    unnamed x1 -> x0, blocking collectives: 29.6 us -> none
    dot_general x8 -> x0, matrix products: 27.1 us -> none  [the longest x1 8.59 us: prefill(): jnp.einsum('td,dkc->tkc', columns, lax.all_gather(kv_weight1, 'engine', a...]
    convert_element_type x5 -> x1, local copies, waits for them, and re-layouts: 26.3 us -> 0.09 us  [body(): slot = jnp.cumsum(here.astype(jnp.int32)) - 1]
    reduce_sum x5 -> x0, other arithmetic: 13.2 us -> none  [the longest x4 13 us: root_norm(): jnp.mean(values * values, axis=-1, keepdims=True) + NORM_EPSILON]
    all_to_all x1 -> x0, starting transfers between devices: 12.9 us -> none  [body(): lax.all_to_all(outgoing, 'engine', split_axis=0, concat_axis=0, tiled=True)]
  transfers between devices with their start and end apart: 7 -> 0, of which waited for: 6 -> 0; matrix products, arithmetic and copies ran while one was open for 10% -> 0% of each run, Pallas kernels for 0% -> 0%
where the time goes in v1:
time: 155 us
  Pallas kernels  145 us (94%)
  local copies, waits for them, and re-layouts  7 us (5%)
  other arithmetic  3.06 us (2%)
    pallas_call x1, Pallas kernels, body(): pl.pallas_call(mega, out_shape=(jax.ShapeDtypeStruct((32, 16, 640), BF),...  144 us
    unnamed x17, local copies, waits for them, and re-layouts  3.71 us

profile of v1, /device:TPU:39, one launch (start us, length us, event | category | flops | bytes accessed | tf_op | source)
XLA Modules:
  0.0 154.9 jit_solution(6959415185947277461)
XLA Ops:
  0.0 0.0 copy-start.2
  0.0 0.0 copy-start.3
  0.0 0.9 copy.25
  1.0 0.9 copy.26
  1.9 0.0 copy-done.2
  1.9 0.0 copy-done.3
  1.9 0.0 copy-start.4
  1.9 0.0 copy-start.1
  1.9 0.8 pad_maximum_fusion
  2.7 0.0 copy-done.4
  2.7 0.6 slice_reduce_fusion
  3.4 0.7 reshape_squeeze.7.g1
  4.1 0.0 copy-done.1
  4.1 0.1 copy.18
  4.2 0.8 reshape.77.x_in
  5.0 0.0 copy-start.5
  5.0 0.0 copy-start.6
  5.0 0.6 copy-done.5
  5.6 0.0 copy-done.6
  5.7 0.6 add_bitcast_fusion.info_in
  6.3 144.1 %prefill.1 = (bf16[32,16,640]{2,1,0:T(8,128)(2,1)}, s32[32,1,128]{2,1,0:T(1,128)}) custom-call(bf16[320,640]{1,0:T(8,128)(2,1)} %reshape.77.x_in, bf16[160,768]{1,0:T(8,128)(2,1)} %get-tuple-element.11.wq_in, bf16[160,768]{1,0:T(8,128)(2,1)} %get-tuple-element.12.wo_in, s32[1,128]{1,0:T(1,128)} %add_bitcast_fusion.info_in, f32[8,1,640]{2,1,0:T(1,128)} %bitcast.20, ...), custom_call_target="tpu_custom_call" | custom-call | tf_op jit(solution)/shard_map/prefill/pallas_call | solution.py:599
  150.4 1.4 compare_reduce_fusion
  151.8 0.1 copy.19
  151.9 0.1 reduce-window.8
  152.0 0.1 multiply_reduce_fusion
  152.1 0.1 iota_add_fusion
  152.2 0.1 add.32.key
  152.3 0.0 copy-start
  152.3 1.1 copy-done
  153.4 0.6 place_rows.1
  153.9 0.9 copy.20
  (3 shorter events, 0.0 us)
Async XLA Ops:
  0.0 1.9 %copy-start.2 = (bf16[160,512]{1,0:T(8,128)(2,1)S(1)}, bf16[160,512]{1,0:T(8,128)(2,1)}, u32[]{:S(2)}) copy-start(bf16[160,512]{1,0:T(8,128)(2,1)} %param.20) | copy-start | bytes 491524
  0.0 1.9 %copy-start.3 = (bf16[160,512]{1,0:T(8,128)(2,1)S(1)}, bf16[160,512]{1,0:T(8,128)(2,1)}, u32[]{:S(2)}) copy-start(bf16[160,512]{1,0:T(8,128)(2,1)} %param.22) | copy-start | bytes 491524
  1.9 0.8 copy-start.4
  1.9 2.2 %copy-start.1 = (bf16[16,20,640]{2,0,1:T(8,128)(2,1)S(1)}, bf16[16,20,640]{2,0,1:T(8,128)(2,1)}, u32[]{:S(2)}) copy-start(bf16[16,20,640]{2,0,1:T(8,128)(2,1)} %param.14) | copy-start | bytes 1228804
  5.0 0.7 copy-start.5
  5.0 0.7 copy-start.6
  152.3 1.1 copy-start

commit v2 on v1

v2 whole, which is shorter than its diff:
```python
import functools

import jax
import jax.numpy as jnp
import numpy as np
from jax import lax
from jax.experimental import pallas as pl
from jax.experimental.pallas import tpu as pltpu
from jax.sharding import PartitionSpec as P

EPS = 1e-06
ROTARY_BASE = 1000000.0
MESH = pl.DeviceIdType.MESH
TOK = 320
SPAN = 20
WC = 768
CB = 80
F32 = jnp.float32
BF = jnp.bfloat16
NT = (((1,), (1,)), ((), ()))


def mod4(v):
    return lax.rem(v + 8, 4)


def device(x, y, z, c):
    z = lax.rem(z + 16, 8)
    return (mod4(x) * 8 + (z // 4) * 4 + mod4(y), lax.rem(z, 4) * 2 + c)


def rcopy(src, dst, send_sem, recv_sem, target):
    return pltpu.make_async_remote_copy(
        src_ref=src, dst_ref=dst, send_sem=send_sem, recv_sem=recv_sem,
        device_id=target, device_id_type=MESH,
    )


def rope(v, cos, sin):
    return v * cos + pltpu.roll(v, 64, 1) * sin


def head_norm(v, gain):
    return v * lax.rsqrt(jnp.mean(v * v, axis=1, keepdims=True) + EPS) * gain


class Gather:
    def __init__(self, buf, slot, me, ssem, rsem):
        self.buf, self.slot, self.me = buf, slot, me
        self.ssem, self.rsem = ssem, rsem
        self.sent = []

    def place(self, h, i, j, core=None):
        x, y, z, c = self.me
        c = c if core is None else core
        if h == 0:
            return self.slot(mod4(x + i), mod4(y + j), c)
        return self.slot(mod4(x + j), mod4(y + i), c)

    def to(self, h, axis, step):
        x, y, z, c = self.me
        if (h == 0) == (axis == 0):
            return device(x + step, y, z, c)
        return device(x, y + step, z, c)

    def view(self, slot, h, cols):
        return self.buf.at[slot, pl.ds(80 * h, 80), cols]

    def send(self, h, i, j, cols, target, k):
        ref = self.view(self.place(h, i, j), h, cols)
        cp = rcopy(ref, ref, self.ssem.at[h, k], self.rsem.at[h, k], target)
        cp.start()
        self.sent.append(cp)

    def recv(self, h, i, j, cols, k, core=None):
        ref = self.view(self.place(h, i, j, core), h, cols)
        rcopy(ref, ref, self.ssem.at[h, k], self.rsem.at[h, k], self.to(h, 0, 1)).wait_recv()

    ALL = slice(0, WC)
    LEFT = slice(0, WC // 2)
    RIGHT = slice(WC // 2, WC)
    OFF = (0, -1, 1, 2)

    def sibling(self, h, ii, jj):
        x, y, z, c = self.me
        self.send(h, self.OFF[ii], self.OFF[jj], self.ALL, device(x, y, z, 1 - c), 20 + 4 * ii + jj)

    def first(self):
        for h in range(2):
            self.send(h, 0, 0, self.ALL, self.to(h, 0, 1), 0)
            self.send(h, 0, 0, self.ALL, self.to(h, 0, -1), 1)
        for h in range(2):
            self.second_send(h, 0)
            self.sibling(h, 0, 0)

    def first_drain(self):
        for h in range(2):
            for k, cols in ((0, self.ALL), (1, self.ALL), (4, self.ALL), (5, self.ALL), (20, self.ALL)):
                ref = self.view(self.place(h, 0, 0), h, cols)
                rcopy(ref, ref, self.ssem.at[h, k], self.rsem.at[h, k], self.to(h, 0, 1)).wait_send()

    def first_recv(self):
        for h in range(2):
            self.recv(h, -1, 0, self.ALL, 0)
            self.send(h, -1, 0, self.LEFT, self.to(h, 0, 1), 2)
            self.recv(h, 1, 0, self.ALL, 1)
            self.send(h, 1, 0, self.RIGHT, self.to(h, 0, -1), 3)
        for h in range(2):
            self.second_send(h, 1)
            self.second_send(h, 2)
            self.sibling(h, 1, 0)
            self.sibling(h, 2, 0)

    def first_last(self):
        for h in range(2):
            self.recv(h, 2, 0, self.LEFT, 2)
            self.recv(h, 2, 0, self.RIGHT, 3)
            self.second_send(h, 3)
            self.sibling(h, 3, 0)

    def second_send(self, h, ii):
        i = self.OFF[ii]
        self.send(h, i, 0, self.ALL, self.to(h, 1, 1), 4 + 2 * ii)
        self.send(h, i, 0, self.ALL, self.to(h, 1, -1), 5 + 2 * ii)

    def second_recv(self, ii):
        i = self.OFF[ii]
        for h in range(2):
            self.recv(h, i, -1, self.ALL, 4 + 2 * ii)
            self.send(h, i, -1, self.LEFT, self.to(h, 1, 1), 12 + 2 * ii)
            self.recv(h, i, 1, self.ALL, 5 + 2 * ii)
            self.send(h, i, 1, self.RIGHT, self.to(h, 1, -1), 13 + 2 * ii)
            self.sibling(h, ii, 1)
            self.sibling(h, ii, 2)

    def second_last(self, ii):
        i = self.OFF[ii]
        for h in range(2):
            self.recv(h, i, 2, self.LEFT, 12 + 2 * ii)
            self.recv(h, i, 2, self.RIGHT, 13 + 2 * ii)
            self.sibling(h, ii, 3)

    def finish(self):
        c = self.me[3]
        for h in range(2):
            for ii in range(4):
                for jj in range(4):
                    self.recv(h, self.OFF[ii], self.OFF[jj], self.ALL, 20 + 4 * ii + jj, 1 - c)

    def drain(self):
        for cp in self.sent:
            cp.wait_send()
        self.sent = []


class Ring:
    LONG = {1: (0, 1), -1: (2, 3)}

    def __init__(self, buf, slot, me, ssem, rsem):
        self.buf, self.slot, self.me = buf, slot, me
        self.ssem, self.rsem = ssem, rsem
        self.sent = []

    def order(self, k):
        lo, sh = self.LONG[1], self.LONG[-1]
        if k == 4:
            return ((1, lo[0]), (-1, sh[0]), (1, lo[1]), (-1, sh[1]))
        return ((1, lo[0]), (-1, sh[0]), (1, sh[0]), (-1, lo[0]),
                (1, lo[1]), (-1, sh[1]), (1, sh[1]), (-1, lo[1]))

    def view(self, origin, part):
        return self.buf.at[self.slot(lax.rem(origin + 16, 8)), pl.ds(80 * part, 80)]

    def send(self, way, part, k, src=None):
        x, y, z, c = self.me
        d = 0 if way > 0 else 1
        ref = self.view(z - way * (k - 1), part)
        cp = rcopy(ref if src is None else src, ref, self.ssem.at[d, part, k - 1],
                   self.rsem.at[d, part, k - 1], device(x, y, z + way, c))
        cp.start()
        self.sent.append(cp)

    def recv(self, way, part, k):
        x, y, z, c = self.me
        d = 0 if way > 0 else 1
        ref = self.view(z - way * k, part)
        rcopy(ref, ref, self.ssem.at[d, part, k - 1], self.rsem.at[d, part, k - 1],
              device(x, y, z + way, c)).wait_recv()
        if k < 3 or (k == 3 and part in self.LONG[way]):
            self.send(way, part, k + 1)

    def drain(self):
        for cp in self.sent:
            cp.wait_send()
        self.sent = []


def mega(tok_in, q_in, kv0_in, out_in, kv1_in, dest_in, len_in, gains_in, qg_in, kg_in,
         cos_in, sin_in, mask_in, lanes_in, caches,
         XS, KV0, KV1, DEST, LEN, gains, qg, kg, cos, sin, mask, lanes, land0, land1, info_land, OUT,
         WQS, WOS, XX, WQ, WO, A, ACC, HID, HB, PP, RSS, RSR, SS, SEND0, SEND1, VAL, INFO, MY,
         in_sem, own_sem, out_sem, swap_s, swap_r, xs, xr, xcs, xcr, wqs, wqr, ts, tr, wos, wor,
         as_, ar, rss, rsr, sss, ssr, es, er, fs, fr, ns, nr):
    e = lax.axis_index("engine")
    t = lax.axis_index("tensor")
    x, y, a = e // 8, lax.rem(e, 4), lax.rem(e // 4, 2)
    zl, c = t // 2, lax.rem(t, 2)
    z = a * 4 + zl
    me = (x, y, z, c)
    sib = device(x, y, z, 1 - c)
    partner = device(x, y, z + 4, 1 - c)
    moved = a != c

    def t_to(u):
        return device(x, zl + 1, a * 4 + 2 * u + lax.rem(y, 2), c)

    def t_from(yhi):
        return device(x, 2 * yhi + lax.rem(zl, 2), a * 4 + mod4(y - 1), c)

    bar = pltpu.get_barrier_semaphore()
    for other in (device(x + 1, y, z, c), device(x - 1, y, z, c), device(x, y + 1, z, c),
                  device(x, y - 1, z, c), device(x, y, z + 1, c), device(x, y, z - 1, c),
                  sib, partner, t_to(0), t_to(1), t_from(0), t_from(1)):
        pl.semaphore_signal(bar, inc=1, device_id=other, device_id_type=MESH)

    fetch = {}
    for n, (src, dst) in enumerate((
            (tok_in, XS), (kv0_in, KV0), (dest_in, DEST), (len_in, LEN), (kv1_in, KV1),
            (gains_in, gains), (qg_in, qg), (kg_in, kg), (cos_in, cos), (sin_in, sin),
            (mask_in, mask), (lanes_in, lanes))):
        fetch[n] = pltpu.make_async_copy(src, dst, in_sem.at[n])
        fetch[n].start()
    q_copy = pltpu.make_async_copy(q_in, WQS.at[:, pl.ds(0, 512)], own_sem.at[0])
    out_copy = pltpu.make_async_copy(out_in, WOS.at[:, pl.ds(0, 512)], own_sem.at[1])
    q_copy.start()
    out_copy.start()
    for n in (1, 2, 3):
        fetch[n].wait()
    for kind in range(2):
        WQS[:, 512 + 128 * kind:640 + 128 * kind] = KV0[:, kind, :]
    MY[...] = jnp.zeros_like(MY)
    MY[:, 0:16] = DEST[...]
    MY[:, 16:32] = LEN[...]
    q_copy.wait()
    fetch[0].wait()
    pl.semaphore_wait(bar, 12)

    def x_slot(origin):
        oa, ol = origin // 4, lax.rem(origin, 4)
        return jnp.where(oa == c, 2 * ol + c, 8 + ol)

    def wq_slot(sx, sy, sc):
        return sx * 8 + sc * 4 + sy

    def wo_slot(sx, sy, sc):
        return (2 * mod4(sy - 1) + sc) * 4 + sx

    swap_slot = x * 8 + a * 4 + y

    def swap_copies():
        return (
            rcopy(WQS, WQ.at[swap_slot], swap_s.at[0], swap_r.at[0], partner),
            rcopy(MY, INFO, swap_s.at[1], swap_r.at[1], partner),
        )

    def stay_copies():
        return (
            pltpu.make_async_copy(WQS, WQ.at[swap_slot], swap_r.at[0]),
            pltpu.make_async_copy(MY, INFO, swap_r.at[1]),
        )

    gq = Gather(WQ, wq_slot, me, wqs, wqr)
    ring = Ring(XX, x_slot, me, xs, xr)

    @pl.when(moved)
    def _():
        for cp in swap_copies():
            cp.start()

    @pl.when(jnp.logical_not(moved))
    def _():
        for cp in stay_copies():
            cp.start()

    for way, part in ring.order(1):
        ring.send(way, part, 1, XS.at[pl.ds(80 * part, 80)])
    own_x = pltpu.make_async_copy(XS, XX.at[x_slot(z)], own_sem.at[2])
    own_x.start()

    @pl.when(jnp.logical_not(moved))
    def _():
        for cp in stay_copies():
            cp.wait()
        gq.first()

    gq.sent = []
    def x_cross(origin, part, src=None):
        origin = lax.rem(origin + 16, 8)
        oa, ol = origin // 4, lax.rem(origin, 4)

        @pl.when(oa != c)
        def _():
            rows = pl.ds(80 * part, 80)
            rcopy(XX.at[8 + ol, rows] if src is None else src, XX.at[2 * ol + c, rows],
                  xcs.at[ol, part], xcr.at[ol, part], sib).start()

    def x_crossed(ol):
        for part in range(4):
            rows = pl.ds(80 * part, 80)
            rcopy(XX.at[8 + ol, rows], XX.at[2 * ol + 1 - c, rows],
                  xcs.at[ol, part], xcr.at[ol, part], sib).wait_recv()

    def x_recv(k, low=0, high=8):
        for way, part in ring.order(k)[low:high]:
            ring.recv(way, part, k)
            x_cross(z - way * k, part)

    for part in range(4):
        x_cross(z, part, XS.at[pl.ds(80 * part, 80)])

    fetch[4].wait()
    for kind in range(2):
        WOS[:, 512 + 128 * kind:640 + 128 * kind] = KV1[:, kind, :]
    x_recv(1, 0, 4)

    @pl.when(moved)
    def _():
        for cp in swap_copies():
            cp.wait()
        gq.first()

    gq.sent = []
    x_recv(1, 4, 8)
    x_recv(2, 0, 4)
    gq.first_recv()
    x_recv(2, 4, 8)
    out_copy.wait()

    def shift(u):
        return rcopy(WOS.at[pl.ds(80 * u, 80)],
                     WO.at[(2 * zl + c) * 4 + x, pl.ds(80 * (y // 2), 80)],
                     ts.at[u], tr.at[y // 2], t_to(u))

    for u in range(2):
        shift(u).start()
    gq.first_last()
    gq.second_recv(0)
    x_recv(3, 0, 4)
    gq.second_recv(1)
    gq.second_recv(2)
    gq.second_last(0)
    x_recv(3, 4, 8)
    gq.second_recv(3)
    gq.second_last(1)
    for yhi in range(2):
        half = WO.at[wo_slot(x, y, c), pl.ds(80 * yhi, 80)]
        rcopy(half, half, ts.at[yhi], tr.at[yhi], sib).wait_recv()
    go = Gather(WO, wo_slot, me, wos, wor)
    go.first()
    gq.second_last(2)
    gq.second_last(3)
    gq.finish()
    own_x.wait()

    for n in range(5, 12):
        fetch[n].wait()

    ACC[...] = jnp.zeros_like(ACC)

    def qkv_step(i, total):
        xv = XX[i].astype(F32)
        total = total + jnp.sum(xv * xv, axis=1, keepdims=True)
        xn = (xv * gains[0:1, pl.ds(pl.multiple_of(640 * i, 128), 640)]).astype(BF)
        w = WQ[pl.ds(4 * i, 4)].reshape(640, WC)
        ACC[...] += jnp.dot(xn, w, preferred_element_type=F32)
        return total

    for n in range(1, 4):
        x_crossed(lax.rem(zl + n, 4))
    total = lax.fori_loop(
        0, 6, lambda j, s: qkv_step(2 * lax.rem(zl + 1 + j // 2, 4) + lax.rem(j, 2), s),
        jnp.zeros((TOK, 1), F32))
    x_recv(4, 0, 4)
    go.first_recv()
    x_crossed(zl)
    total = lax.fori_loop(0, 2, lambda j, s: qkv_step(2 * zl + j, s), total)
    r0 = lax.rsqrt(total / 5120.0 + EPS)
    cosv, sinv = cos[...], sin[...]
    VAL[:, 0:128] = rope(head_norm(ACC[:, 512:640] * r0, kg[0:1]), cosv, sinv).astype(BF)
    VAL[:, 128:256] = (ACC[:, 640:768] * r0).astype(BF)
    for g in range(4):
        cols = slice(128 * g, 128 * g + 128)
        A[z, :, cols] = rope(head_norm(ACC[:, cols] * r0, qg[...]), cosv, sinv).astype(BF)
    go.first_last()
    att = Ring(A, lambda origin: origin, me, as_, ar)
    for n in (0, 2, 1, 3):
        rows = slice(CB * n, CB * n + CB)
        keys = slice(0, CB * n + CB)
        q = jnp.concatenate([A[z, rows, 128 * g:128 * g + 128] for g in range(4)], axis=0)
        s = lax.dot_general(q, VAL[keys, 0:128], NT, preferred_element_type=F32)
        seen = jnp.concatenate([mask[rows, keys]] * 4, axis=0)
        w = jnp.where(seen > 0, jnp.exp(s / jnp.sqrt(F32(128.0))), 0.0)
        p = (w / jnp.sum(w, axis=1, keepdims=True)).astype(BF)
        o = jnp.dot(p, VAL[keys, 128:256], preferred_element_type=F32).astype(BF)
        for g in range(4):
            A[z, rows, 128 * g:128 * g + 128] = o[CB * g:CB * g + CB]
        att.send(1, n, 1)
        att.send(-1, n, 1)

    def att_recv(k, low=0, high=8):
        for way, part in att.order(k)[low:high]:
            att.recv(way, part, k)

    go.second_recv(0)

    info = jnp.broadcast_to(INFO[...].astype(F32), (8, 128)).astype(BF)
    lane = lax.broadcasted_iota(jnp.int32, (128, TOK), 0)
    row_of, tok_of = lanes[0:1, :], lanes[1:2, :]
    dest_l = jnp.dot(info, (lane == row_of).astype(BF), preferred_element_type=F32)[0:1]
    len_l = jnp.dot(info, (lane == row_of + 16).astype(BF), preferred_element_type=F32)[0:1]
    dest_l = dest_l.astype(jnp.int32)
    live = tok_of < len_l.astype(jnp.int32)
    key_a = jnp.where(jnp.logical_and(live, tok_of < 16), dest_l * 16 + tok_of, -1000)
    key_b = jnp.where(jnp.logical_and(live, tok_of >= 16), dest_l * 16 + tok_of - 16, -1000)
    place = lax.broadcasted_iota(jnp.int32, (512, TOK), 0)

    def head_rows(cols):
        return jnp.dot((place == key_a).astype(BF), VAL[:, cols], preferred_element_type=F32)

    def tail_rows(f):
        return jnp.dot((place == key_b + 4 * f).astype(BF), VAL[:, 128 * f:128 * f + 128],
                       preferred_element_type=F32)

    SEND0[...] = head_rows(slice(0, 256)).astype(BF).reshape(32, 16, 256)
    tail = tail_rows(0) + tail_rows(1)
    SEND1[:, :, 256:384] = tail.astype(BF).reshape(32, 16, 128)

    pick_row = lax.broadcasted_iota(jnp.int32, (640, 160), 0)
    pick_col = lax.broadcasted_iota(jnp.int32, (640, 160), 1)
    u, v = zl // 2, lax.rem(zl, 2)
    pick = pick_row == pick_col + jnp.where(pick_col >= 80, 240, 0) + (160 * v + 80 * u)
    pick_b, pick_f = pick.astype(BF), pick.astype(F32)
    g1 = []
    for sx in range(4):
        HID[sx] = jnp.dot(XX[2 * sx + a], pick_b, preferred_element_type=F32)
        at = 1280 * sx
        gv = jnp.where(a == 0, gains[1:2, at:at + 640], gains[1:2, at + 640:at + 1280])
        g1.append(jnp.dot(jnp.broadcast_to(gv, (8, 640)), pick_f, preferred_element_type=F32,
                          precision=lax.Precision.HIGHEST)[0:1])

    mine = x * 8 + c * 4 + y

    def target(d):
        return (d, 2 * zl + a)

    def same(d):
        return jnp.logical_and(d == e, a == c)

    def hand_out(srcs):
        def step(d, carry):
            @pl.when(same(d))
            def _():
                for src, dst, ss, rs in srcs(d):
                    pltpu.make_async_copy(src, dst, rs.at[mine]).start()

            @pl.when(jnp.logical_not(same(d)))
            def _():
                for src, dst, ss, rs in srcs(d):
                    rcopy(src, dst, ss.at[d], rs.at[mine], target(d)).start()
            return carry

        lax.fori_loop(0, 32, step, 0)

    def early(d):
        return ((INFO, info_land.at[mine], ns, nr), (SEND0.at[d], land0.at[mine], es, er))

    def late(d):
        return ((SEND1.at[d], land1.at[mine], fs, fr),)

    def out_step(origin):
        origin = lax.rem(origin + 16, 8)
        head = 2 * lax.rem(origin, 4) + origin // 4
        for sx in range(4):
            part = lax.dot_general(A[origin], WO[head * 4 + sx, :, 0:512], NT,
                                   preferred_element_type=F32)
            HID[sx] += part.astype(BF).astype(F32)

    att_recv(1)
    go.second_recv(1)
    go.second_recv(2)
    att_recv(2, 0, 4)
    go.second_last(0)
    go.second_recv(3)
    att_recv(2, 4, 8)
    go.second_last(1)
    go.second_last(2)
    att_recv(3, 0, 4)
    go.second_last(3)
    att_recv(3, 4, 8)
    go.finish()
    hand_out(early)
    for k in (0, -1, 1, -2, 2, -3, 3):
        out_step(z + k)
    att_recv(4, 0, 4)
    out_step(z + 4)

    col = jnp.zeros((TOK, 1), F32)
    for sx in range(4):
        hv = HID[sx]
        col = col + jnp.sum(hv * hv, axis=1, keepdims=True)
        HB[sx] = (hv * g1[sx]).astype(BF)

    def partial(dest):
        dest = lax.rem(dest + 16, 8)
        head = 2 * lax.rem(dest, 4) + dest // 4
        out = jnp.dot(HB[0], WO[head * 4, :, 512:768], preferred_element_type=F32)
        for sx in range(1, 4):
            out = out + jnp.dot(HB[sx], WO[head * 4 + sx, :, 512:768], preferred_element_type=F32)
        PP[dest] = out

    rs_sent = []

    def rs_copy(way, part, s):
        d = 0 if way > 0 else 1
        return rcopy(RSS.at[d, part, s], RSR.at[d, part, s], rss.at[d, part, s],
                     rsr.at[d, part, s], device(x, y, z + way, c))

    def rs_send(way, part, s, value):
        RSS[0 if way > 0 else 1, part, s] = value.astype(BF)
        cp = rs_copy(way, part, s)
        cp.start()
        rs_sent.append(cp)

    def rs_recv(way, part, s):
        rs_copy(way, part, s).wait_recv()
        return RSR[0 if way > 0 else 1, part, s].astype(F32)

    def hops(way, part):
        return 4 if part in Ring.LONG[way] else 3

    def own_part(way, part, s):
        dest = lax.rem(z + way * (hops(way, part) - s) + 16, 8)
        return PP[dest, pl.ds(80 * part, 80)]

    partial(z + 4)
    for way, part in ((1, 0), (-1, 2), (1, 1), (-1, 3)):
        rs_send(way, part, 0, own_part(way, part, 0))
    partial(z + 3)
    partial(z - 3)
    for way, part in ((1, 2), (-1, 0), (1, 3), (-1, 1)):
        rs_send(way, part, 0, own_part(way, part, 0))
    eye = (lax.broadcasted_iota(jnp.int32, (TOK, TOK), 0)
           == lax.broadcasted_iota(jnp.int32, (TOK, TOK), 1))
    SS[z] = jnp.sum(jnp.where(eye, col, 0.0), axis=0, keepdims=True)
    ss_sent = []
    for k in range(1, 8):
        cp = rcopy(SS.at[z], SS.at[z], sss.at[k], ssr.at[k], device(x, y, z + k, c))
        cp.start()
        ss_sent.append(cp)
    for k in (2, -2, 1, -1, 0):
        partial(z + k)
    ring_order = ((1, 0), (-1, 2), (1, 1), (-1, 3), (1, 2), (-1, 0), (1, 3), (-1, 1))
    for s in range(3):
        for way, part in ring_order:
            if s < hops(way, part) - 1:
                rs_send(way, part, s + 1, rs_recv(way, part, s) + own_part(way, part, s + 1))
    ss_total = SS[z]
    for k in range(1, 8):
        origin = lax.rem(z - k + 16, 8)
        rcopy(SS.at[origin], SS.at[origin], sss.at[k], ssr.at[k], device(x, y, z + k, c)).wait_recv()
        ss_total = ss_total + SS[origin]
    r1 = lax.rsqrt(jnp.sum(jnp.where(eye, ss_total, 0.0), axis=1, keepdims=True) / 5120.0 + EPS)

    for part in range(4):
        way = 1 if part in Ring.LONG[1] else -1
        rows = slice(80 * part, 80 * part + 80)
        kv = PP[z, rows] + rs_recv(-way, part, 2) + rs_recv(way, part, 3)
        kv = kv * r1[rows]
        VAL[rows, 256:384] = rope(head_norm(kv[:, 0:128], kg[1:2]), cos[rows], sin[rows]).astype(BF)
        VAL[rows, 384:512] = kv[:, 128:256].astype(BF)

    SEND1[:, :, 0:256] = head_rows(slice(256, 512)).astype(BF).reshape(32, 16, 256)
    tail = tail + tail_rows(2) + tail_rows(3)
    SEND1[:, :, 256:384] = tail.astype(BF).reshape(32, 16, 128)
    hand_out(late)

    def landed(srcs, dsts):
        def step(d, carry):
            for (src, _, ss, rs), dst in zip(srcs(d), dsts):
                rcopy(src, dst.at[d], ss.at[d], rs.at[d], target(d)).wait_recv()

            @pl.when(jnp.logical_not(same(d)))
            def _():
                for (src, _, ss, rs), dst in zip(srcs(d), dsts):
                    rcopy(src, dst.at[d], ss.at[d], rs.at[d], target(d)).wait_send()
            return carry

        lax.fori_loop(0, 32, step, 0)

    for part in (ring, gq, go, att):
        part.drain()
    for cp in ss_sent + rs_sent:
        cp.wait_send()
    for u in range(2):
        shift(u).wait_send()
    gq.first_drain()
    for ol in range(4):
        for part in range(4):
            rows = pl.ds(80 * part, 80)
            rcopy(XX.at[8 + ol, rows], XX.at[2 * ol + c, rows],
                  xcs.at[ol, part], xcr.at[ol, part], sib).wait_send()

    landed(early, (info_land, land0))
    lane = lax.broadcasted_iota(jnp.int32, (32, 128), 1)
    hit = jnp.logical_and(info_land[...].reshape(32, 128) == e, lane < 16)
    here = jnp.max(hit.astype(F32), axis=1, keepdims=True)
    before = (lax.broadcasted_iota(jnp.int32, (32, 32), 1)
              < lax.broadcasted_iota(jnp.int32, (32, 32), 0)).astype(BF)
    rank = jnp.dot(before, jnp.broadcast_to(here, (32, 128)).astype(BF), preferred_element_type=F32)
    key = jnp.where(here > 0, rank[:, 0:1], -1000.0)
    key = jnp.broadcast_to(key[:, None, :], (32, 16, 512))
    row = lax.broadcasted_iota(jnp.int32, (32, 16, 512), 1).astype(F32) * 32.0
    at = lax.broadcasted_iota(jnp.int32, (32, 16, 512), 2).astype(F32)
    pick_rows = (key + row == at).astype(BF).reshape(512, 512)
    tn = (((0,), (0,)), ((), ()))

    def settle(block):
        out = lax.dot_general(pick_rows, block, tn, preferred_element_type=F32)
        return out.astype(BF).reshape(16, 32, block.shape[1])

    rows0 = settle(land0[...].reshape(512, 256))
    for f in range(2):
        OUT[f, 0:16] = rows0[:, :, 128 * f:128 * f + 128]
    landed(late, (land1,))
    rows1 = settle(land1[...].reshape(512, 384))
    for f in range(2):
        OUT[2 + f, 0:16] = rows1[:, :, 128 * f:128 * f + 128]
    for f in range(4):
        OUT[f, 16:20] = rows1[4 * f:4 * f + 4, :, 256:384]
    put = pltpu.make_async_copy(OUT, caches, out_sem)
    put.start()
    put.wait()


def tables():
    half = 64
    where = np.arange(TOK) // 16
    pos = where.astype(np.float32)
    freq = np.power(ROTARY_BASE, -np.arange(half, dtype=np.float64) * 2.0 / 128).astype(np.float32)
    angle = (pos[:, None] * freq[None, :]).astype(np.float32).astype(np.float64)
    cos, sin = np.cos(angle), np.sin(angle)
    cos = np.concatenate([cos, cos], axis=1).astype(np.float32)
    sin = np.concatenate([-sin, sin], axis=1).astype(np.float32)
    i, j = np.arange(TOK)[:, None], np.arange(TOK)[None, :]
    mask = ((i % 16 == j % 16) & (j <= i)).astype(np.float32)
    lanes = np.zeros((8, TOK), np.int32)
    lanes[0] = np.arange(TOK) % 16
    lanes[1] = where
    return cos, sin, mask, lanes


def body(token_states, row_len, row_dest, norm_gain, q_gain, k_gain,
         q_weight, kv_weight0, out_weight, kv_weight1):
    cos, sin, mask, lanes = tables()
    hbm = pl.BlockSpec(memory_space=pl.ANY)
    dma = pltpu.SemaphoreType.DMA
    vmem = pltpu.VMEM
    out = pl.pallas_call(
        mega,
        out_shape=jax.ShapeDtypeStruct((4, SPAN, 32, 128), BF),
        in_specs=[hbm] * 14,
        out_specs=hbm,
        scratch_shapes=[
            vmem((TOK, 640), BF), vmem((160, 2, 128), BF), vmem((160, 2, 128), BF),
            vmem((1, 16), jnp.int32), vmem((1, 16), jnp.int32),
            vmem((2, 5120), F32), vmem((1, 128), F32), vmem((2, 128), F32),
            vmem((TOK, 128), F32), vmem((TOK, 128), F32), vmem((TOK, TOK), F32), vmem((8, TOK), jnp.int32),
            vmem((32, 16, 256), BF), vmem((32, 16, 384), BF), vmem((32, 1, 128), jnp.int32),
            vmem((4, SPAN, 32, 128), BF),
            vmem((160, WC), BF), vmem((160, WC), BF),
            vmem((12, TOK, 640), BF), vmem((32, 160, WC), BF), vmem((32, 160, WC), BF),
            vmem((8, TOK, 512), BF), vmem((TOK, WC), F32),
            vmem((4, TOK, 160), F32), vmem((4, TOK, 160), BF), vmem((8, TOK, 256), F32),
            vmem((2, 4, 4, 80, 256), BF), vmem((2, 4, 4, 80, 256), BF), vmem((8, 1, TOK), F32),
            vmem((32, 16, 256), BF), vmem((32, 16, 384), BF), vmem((TOK, 512), BF),
            vmem((1, 128), jnp.int32), vmem((1, 128), jnp.int32),
            dma((12,)), dma((3,)), dma, dma((2,)), dma((2,)),
            dma((2, 4, 4)), dma((2, 4, 4)), dma((4, 4)), dma((4, 4)),
            dma((2, 36)), dma((2, 36)), dma((2,)), dma((2,)), dma((2, 36)), dma((2, 36)),
            dma((2, 4, 4)), dma((2, 4, 4)), dma((2, 4, 4)), dma((2, 4, 4)),
            dma((8,)), dma((8,)), dma((32,)), dma((32,)), dma((32,)), dma((32,)),
            dma((32,)), dma((32,)),
        ],
        compiler_params=pltpu.CompilerParams(
            collective_id=0, has_side_effects=True, vmem_limit_bytes=58 * 2**20),
        name="prefill",
    )(token_states.transpose(1, 0, 2).reshape(TOK, 640), q_weight, kv_weight0, out_weight, kv_weight1,
      row_dest.reshape(1, 16), row_len.reshape(1, 16),
      norm_gain, q_gain.reshape(1, 128), k_gain,
      jnp.asarray(cos), jnp.asarray(sin), jnp.asarray(mask), jnp.asarray(lanes))
    return out.reshape(2, 2, SPAN, 32, 128).transpose(0, 1, 3, 2, 4)


def solution(mesh):
    in_specs = (
        P("engine", None, "tensor"), P("engine"), P("engine"), P(), P(), P(),
        P("engine", "tensor"), P("engine", None, "tensor"),
        P("engine", "tensor"), P("engine", None, "tensor"),
    )
    out_specs = P(None, None, "engine", None, "tensor")
    return jax.shard_map(body, mesh=mesh, in_specs=in_specs, out_specs=out_specs, check_vma=False)
```

time: 155 us -> 135 us (0.87); the launches traced: 155 us -> 133 us
  Pallas kernels: 145 us -> 131 us
  local copies, waits for them, and re-layouts: 7 us -> 1.98 us
  other arithmetic: 3.06 us -> 0 us
    pallas_call x2 -> x1, Pallas kernels: 145 us -> 131 us  [body(): pl.pallas_call(mega, out_shape=jax.ShapeDtypeStruct((4, SPAN, 32, 128), B...]
    reshape x2 -> x0, local copies, waits for them, and re-layouts: 1.77 us -> none  [the longest x1 0.94 us: body(): return out.reshape(2, 2, 32, SPAN, 128)]
    unnamed x17 -> x1, local copies, waits for them, and re-layouts: 3.71 us -> 1.98 us
where the time goes in v2:
time: 135 us; the launch traced here: 133 us
  Pallas kernels  131 us (97%)
  local copies, waits for them, and re-layouts  1.98 us (1%)
    pallas_call x1, Pallas kernels, body(): pl.pallas_call(mega, out_shape=jax.ShapeDtypeStruct((4, SPAN, 32, 128), B...  131 us

profile of v2, /device:TPU:39, one launch (start us, length us, event | category | flops | bytes accessed | tf_op | source)
XLA Modules:
  0.0 133.1 jit_solution(13852576132564839618)
XLA Ops:
  0.0 131.1 %prefill.1 = bf16[4,20,32,128]{3,2,1,0:T(8,128)(2,1)} custom-call(bf16[320,640]{1,0:T(8,128)(2,1)} %bitcast.10, bf16[160,512]{1,0:T(8,128)(2,1)} %q_in.1, bf16[160,2,128]{2,1,0:T(2,128)(2,1)} %kv0_in.1, bf16[160,512]{1,0:T(8,128)(2,1)} %out_in.1, bf16[160,2,128]{2,1,0:T(2,128)(2,1)} %kv1_in.1, s32[1,16]{1,0:T(1,128)} %bitcast.11, s32[1,16]{1,0:T(1,128)} %bitcast.12, ...), custom_call_target="tpu_custom_call" | custom-call | tf_op jit(solution)/shard_map/prefill/pallas_call | solution.py:668
  131.1 2.0 %copy.16 = bf16[2,2,32,20,128]{4,2,3,1,0:T(8,128)(2,1)} copy(bf16[2,2,32,20,128]{4,2,3,1,0:T(8,128)(2,1)} %bitcast.9) | data formatting | bytes 1310720

commit v3 on v2

--- a/solution.py
+++ b/solution.py
@@ -45,10 +45,9 @@
 
 
 class Gather:
-    def __init__(self, buf, slot, me, ssem, rsem):
+    def __init__(self, buf, slot, me, ssem, rsem, csem):
         self.buf, self.slot, self.me = buf, slot, me
-        self.ssem, self.rsem = ssem, rsem
-        self.sent = []
+        self.ssem, self.rsem, self.csem = ssem, rsem, csem
 
     def place(self, h, i, j, core=None):
         x, y, z, c = self.me
@@ -68,13 +67,12 @@
 
     def send(self, h, i, j, cols, target, k):
         ref = self.view(self.place(h, i, j), h, cols)
-        cp = rcopy(ref, ref, self.ssem.at[h, k], self.rsem.at[h, k], target)
-        cp.start()
-        self.sent.append(cp)
-
-    def recv(self, h, i, j, cols, k, core=None):
-        ref = self.view(self.place(h, i, j, core), h, cols)
-        rcopy(ref, ref, self.ssem.at[h, k], self.rsem.at[h, k], self.to(h, 0, 1)).wait_recv()
+        arrive = self.rsem.at[h, k] if k < 20 else self.csem
+        rcopy(ref, ref, self.ssem, arrive, target).start()
+
+    def recv(self, h, i, j, cols, k):
+        ref = self.view(self.place(h, i, j), h, cols)
+        rcopy(ref, ref, self.ssem, self.rsem.at[h, k], self.to(h, 0, 1)).wait_recv()
 
     ALL = slice(0, WC)
     LEFT = slice(0, WC // 2)
@@ -92,12 +90,6 @@
         for h in range(2):
             self.second_send(h, 0)
             self.sibling(h, 0, 0)
-
-    def first_drain(self):
-        for h in range(2):
-            for k, cols in ((0, self.ALL), (1, self.ALL), (4, self.ALL), (5, self.ALL), (20, self.ALL)):
-                ref = self.view(self.place(h, 0, 0), h, cols)
-                rcopy(ref, ref, self.ssem.at[h, k], self.rsem.at[h, k], self.to(h, 0, 1)).wait_send()
 
     def first_recv(self):
         for h in range(2):
@@ -140,17 +132,16 @@
             self.recv(h, i, 2, self.RIGHT, 13 + 2 * ii)
             self.sibling(h, ii, 3)
 
+    def whole(self, blocks):
+        x, y, z, c = self.me
+        ref = self.buf.at[pl.ds(0, blocks)]
+        return rcopy(ref, ref, self.ssem, self.csem, device(x, y, z, 1 - c))
+
     def finish(self):
-        c = self.me[3]
-        for h in range(2):
-            for ii in range(4):
-                for jj in range(4):
-                    self.recv(h, self.OFF[ii], self.OFF[jj], self.ALL, 20 + 4 * ii + jj, 1 - c)
+        self.whole(16).wait_recv()
 
     def drain(self):
-        for cp in self.sent:
-            cp.wait_send()
-        self.sent = []
+        self.whole(31).wait_send()
 
 
 class Ring:
@@ -159,7 +150,6 @@
     def __init__(self, buf, slot, me, ssem, rsem):
         self.buf, self.slot, self.me = buf, slot, me
         self.ssem, self.rsem = ssem, rsem
-        self.sent = []
 
     def order(self, k):
         lo, sh = self.LONG[1], self.LONG[-1]
@@ -175,31 +165,29 @@
         x, y, z, c = self.me
         d = 0 if way > 0 else 1
         ref = self.view(z - way * (k - 1), part)
-        cp = rcopy(ref if src is None else src, ref, self.ssem.at[d, part, k - 1],
-                   self.rsem.at[d, part, k - 1], device(x, y, z + way, c))
-        cp.start()
-        self.sent.append(cp)
+        rcopy(ref if src is None else src, ref, self.ssem,
+              self.rsem.at[d, part, k - 1], device(x, y, z + way, c)).start()
 
     def recv(self, way, part, k):
         x, y, z, c = self.me
         d = 0 if way > 0 else 1
         ref = self.view(z - way * k, part)
-        rcopy(ref, ref, self.ssem.at[d, part, k - 1], self.rsem.at[d, part, k - 1],
+        rcopy(ref, ref, self.ssem, self.rsem.at[d, part, k - 1],
               device(x, y, z + way, c)).wait_recv()
         if k < 3 or (k == 3 and part in self.LONG[way]):
             self.send(way, part, k + 1)
 
     def drain(self):
-        for cp in self.sent:
-            cp.wait_send()
-        self.sent = []
+        x, y, z, c = self.me
+        ref = self.buf.at[pl.ds(0, 7)]
+        rcopy(ref, ref, self.ssem, self.rsem.at[0, 0, 0], device(x, y, z + 1, c)).wait_send()
 
 
 def mega(tok_in, q_in, kv0_in, out_in, kv1_in, dest_in, len_in, gains_in, qg_in, kg_in,
          cos_in, sin_in, mask_in, lanes_in, caches,
          XS, KV0, KV1, DEST, LEN, gains, qg, kg, cos, sin, mask, lanes, land0, land1, info_land, OUT,
          WQS, WOS, XX, WQ, WO, A, ACC, HID, HB, PP, RSS, RSR, SS, SEND0, SEND1, VAL, INFO, MY,
-         in_sem, own_sem, out_sem, swap_s, swap_r, xs, xr, xcs, xcr, wqs, wqr, ts, tr, wos, wor,
+         in_sem, own_sem, out_sem, swap_s, swap_r, xs, xr, xcs, xcr, wqs, wqr, wqc, ts, tr, wos, wor, woc,
          as_, ar, rss, rsr, sss, ssr, es, er, fs, fr, ns, nr):
     e = lax.axis_index("engine")
     t = lax.axis_index("tensor")
@@ -222,6 +210,18 @@
                   device(x, y - 1, z, c), device(x, y, z + 1, c), device(x, y, z - 1, c),
                   sib, partner, t_to(0), t_to(1), t_from(0), t_from(1)):
         pl.semaphore_signal(bar, inc=1, device_id=other, device_id_type=MESH)
+
+    def x_slot(origin):
+        oa, ol = origin // 4, lax.rem(origin, 4)
+        return jnp.where(oa == c, 2 * ol + c, 8 + ol)
+
+    ring = Ring(XX, x_slot, me, xs, xr)
+    own_x = pltpu.make_async_copy(XS, XX.at[x_slot(z)], own_sem.at[2])
+
+    def x_first():
+        for way, part in ring.order(1):
+            ring.send(way, part, 1, XS.at[pl.ds(80 * part, 80)])
+        own_x.start()
 
     fetch = {}
     for n, (src, dst) in enumerate((
@@ -245,10 +245,6 @@
     fetch[0].wait()
     pl.semaphore_wait(bar, 12)
 
-    def x_slot(origin):
-        oa, ol = origin // 4, lax.rem(origin, 4)
-        return jnp.where(oa == c, 2 * ol + c, 8 + ol)
-
     def wq_slot(sx, sy, sc):
         return sx * 8 + sc * 4 + sy
 
@@ -269,8 +265,7 @@
             pltpu.make_async_copy(MY, INFO, swap_r.at[1]),
         )
 
-    gq = Gather(WQ, wq_slot, me, wqs, wqr)
-    ring = Ring(XX, x_slot, me, xs, xr)
+    gq = Gather(WQ, wq_slot, me, wqs, wqr, wqc)
 
     @pl.when(moved)
     def _():
@@ -282,10 +277,7 @@
         for cp in stay_copies():
             cp.start()
 
-    for way, part in ring.order(1):
-        ring.send(way, part, 1, XS.at[pl.ds(80 * part, 80)])
-    own_x = pltpu.make_async_copy(XS, XX.at[x_slot(z)], own_sem.at[2])
-    own_x.start()
+    x_first()
 
     @pl.when(jnp.logical_not(moved))
     def _():
@@ -293,7 +285,6 @@
             cp.wait()
         gq.first()
 
-    gq.sent = []
     def x_cross(origin, part, src=None):
         origin = lax.rem(origin + 16, 8)
         oa, ol = origin // 4, lax.rem(origin, 4)
@@ -302,13 +293,10 @@
         def _():
             rows = pl.ds(80 * part, 80)
             rcopy(XX.at[8 + ol, rows] if src is None else src, XX.at[2 * ol + c, rows],
-                  xcs.at[ol, part], xcr.at[ol, part], sib).start()
+                  xcs, xcr.at[ol], sib).start()
 
     def x_crossed(ol):
-        for part in range(4):
-            rows = pl.ds(80 * part, 80)
-            rcopy(XX.at[8 + ol, rows], XX.at[2 * ol + 1 - c, rows],
-                  xcs.at[ol, part], xcr.at[ol, part], sib).wait_recv()
+        rcopy(XX.at[8 + ol], XX.at[2 * ol + 1 - c], xcs, xcr.at[ol], sib).wait_recv()
 
     def x_recv(k, low=0, high=8):
         for way, part in ring.order(k)[low:high]:
@@ -321,47 +309,52 @@
     fetch[4].wait()
     for kind in range(2):
         WOS[:, 512 + 128 * kind:640 + 128 * kind] = KV1[:, kind, :]
-    x_recv(1, 0, 4)
-
-    @pl.when(moved)
-    def _():
-        for cp in swap_copies():
-            cp.wait()
-        gq.first()
-
-    gq.sent = []
-    x_recv(1, 4, 8)
-    x_recv(2, 0, 4)
-    gq.first_recv()
-    x_recv(2, 4, 8)
-    out_copy.wait()
+    def moved_first():
+        @pl.when(moved)
+        def _():
+            for cp in swap_copies():
+                cp.wait()
+            gq.first()
+
 
     def shift(u):
         return rcopy(WOS.at[pl.ds(80 * u, 80)],
                      WO.at[(2 * zl + c) * 4 + x, pl.ds(80 * (y // 2), 80)],
-                     ts.at[u], tr.at[y // 2], t_to(u))
-
-    for u in range(2):
-        shift(u).start()
+                     ts, tr.at[y // 2], t_to(u))
+
+    def shift_start():
+        out_copy.wait()
+        for u in range(2):
+            shift(u).start()
+
+    def shift_recv():
+        for yhi in range(2):
+            half = WO.at[wo_slot(x, y, c), pl.ds(80 * yhi, 80)]
+            rcopy(half, half, ts, tr.at[yhi], sib).wait_recv()
+
+    go = Gather(WO, wo_slot, me, wos, wor, woc)
+    moved_first()
+    x_recv(1, 0, 4)
+    gq.first_recv()
+    x_recv(1, 4, 8)
     gq.first_last()
+    x_recv(2, 0, 4)
     gq.second_recv(0)
-    x_recv(3, 0, 4)
     gq.second_recv(1)
+    x_recv(2, 4, 8)
+    shift_start()
     gq.second_recv(2)
     gq.second_last(0)
-    x_recv(3, 4, 8)
+    x_recv(3, 0, 4)
     gq.second_recv(3)
     gq.second_last(1)
-    for yhi in range(2):
-        half = WO.at[wo_slot(x, y, c), pl.ds(80 * yhi, 80)]
-        rcopy(half, half, ts.at[yhi], tr.at[yhi], sib).wait_recv()
-    go = Gather(WO, wo_slot, me, wos, wor)
+    gq.second_last(2)
+    x_recv(3, 4, 8)
+    gq.second_last(3)
+    shift_recv()
     go.first()
-    gq.second_last(2)
-    gq.second_last(3)
     gq.finish()
     own_x.wait()
-
     for n in range(5, 12):
         fetch[n].wait()
 
@@ -377,13 +370,17 @@
 
     for n in range(1, 4):
         x_crossed(lax.rem(zl + n, 4))
-    total = lax.fori_loop(
-        0, 6, lambda j, s: qkv_step(2 * lax.rem(zl + 1 + j // 2, 4) + lax.rem(j, 2), s),
-        jnp.zeros((TOK, 1), F32))
+    total = jnp.zeros((TOK, 1), F32)
+
+    def some(low, high, total):
+        return lax.fori_loop(
+            low, high, lambda j, s: qkv_step(2 * lax.rem(zl + 1 + j // 2, 4) + lax.rem(j, 2), s), total)
+
+    total = some(0, 6, total)
     x_recv(4, 0, 4)
     go.first_recv()
     x_crossed(zl)
-    total = lax.fori_loop(0, 2, lambda j, s: qkv_step(2 * zl + j, s), total)
+    total = some(6, 8, total)
     r0 = lax.rsqrt(total / 5120.0 + EPS)
     cosv, sinv = cos[...], sin[...]
     VAL[:, 0:128] = rope(head_norm(ACC[:, 512:640] * r0, kg[0:1]), cosv, sinv).astype(BF)
@@ -411,7 +408,8 @@
         for way, part in att.order(k)[low:high]:
             att.recv(way, part, k)
 
-    go.second_recv(0)
+    def go_second_recv_0():
+        go.second_recv(0)
 
     info = jnp.broadcast_to(INFO[...].astype(F32), (8, 128)).astype(BF)
     lane = lax.broadcasted_iota(jnp.int32, (128, TOK), 0)
@@ -431,22 +429,24 @@
         return jnp.dot((place == key_b + 4 * f).astype(BF), VAL[:, 128 * f:128 * f + 128],
                        preferred_element_type=F32)
 
-    SEND0[...] = head_rows(slice(0, 256)).astype(BF).reshape(32, 16, 256)
-    tail = tail_rows(0) + tail_rows(1)
-    SEND1[:, :, 256:384] = tail.astype(BF).reshape(32, 16, 128)
-
-    pick_row = lax.broadcasted_iota(jnp.int32, (640, 160), 0)
-    pick_col = lax.broadcasted_iota(jnp.int32, (640, 160), 1)
-    u, v = zl // 2, lax.rem(zl, 2)
-    pick = pick_row == pick_col + jnp.where(pick_col >= 80, 240, 0) + (160 * v + 80 * u)
-    pick_b, pick_f = pick.astype(BF), pick.astype(F32)
-    g1 = []
-    for sx in range(4):
-        HID[sx] = jnp.dot(XX[2 * sx + a], pick_b, preferred_element_type=F32)
-        at = 1280 * sx
-        gv = jnp.where(a == 0, gains[1:2, at:at + 640], gains[1:2, at + 640:at + 1280])
-        g1.append(jnp.dot(jnp.broadcast_to(gv, (8, 640)), pick_f, preferred_element_type=F32,
-                          precision=lax.Precision.HIGHEST)[0:1])
+    g1, tails = [], []
+
+    def prep():
+        SEND0[...] = head_rows(slice(0, 256)).astype(BF).reshape(32, 16, 256)
+        tail = tail_rows(0) + tail_rows(1)
+        SEND1[:, :, 256:384] = tail.astype(BF).reshape(32, 16, 128)
+        tails.append(tail)
+        pick_row = lax.broadcasted_iota(jnp.int32, (640, 160), 0)
+        pick_col = lax.broadcasted_iota(jnp.int32, (640, 160), 1)
+        u, v = zl // 2, lax.rem(zl, 2)
+        pick = pick_row == pick_col + jnp.where(pick_col >= 80, 240, 0) + (160 * v + 80 * u)
+        pick_b, pick_f = pick.astype(BF), pick.astype(F32)
+        for sx in range(4):
+            HID[sx] = jnp.dot(XX[2 * sx + a], pick_b, preferred_element_type=F32)
+            at = 1280 * sx
+            gv = jnp.where(a == 0, gains[1:2, at:at + 640], gains[1:2, at + 640:at + 1280])
+            g1.append(jnp.dot(jnp.broadcast_to(gv, (8, 640)), pick_f, preferred_element_type=F32,
+                              precision=lax.Precision.HIGHEST)[0:1])
 
     mine = x * 8 + c * 4 + y
 
@@ -458,15 +458,16 @@
 
     def hand_out(srcs):
         def step(d, carry):
+
             @pl.when(same(d))
             def _():
                 for src, dst, ss, rs in srcs(d):
-                    pltpu.make_async_copy(src, dst, rs.at[mine]).start()
+                    pltpu.make_async_copy(src, dst, rs).start()
 
             @pl.when(jnp.logical_not(same(d)))
             def _():
                 for src, dst, ss, rs in srcs(d):
-                    rcopy(src, dst, ss.at[d], rs.at[mine], target(d)).start()
+                    rcopy(src, dst, ss, rs, target(d)).start()
             return carry
 
         lax.fori_loop(0, 32, step, 0)
@@ -485,24 +486,29 @@
                                    preferred_element_type=F32)
             HID[sx] += part.astype(BF).astype(F32)
 
-    att_recv(1)
+    go_second_recv_0()
+    att_recv(1, 0, 2)
     go.second_recv(1)
+    att_recv(1, 2, 8)
     go.second_recv(2)
-    att_recv(2, 0, 4)
+    prep()
+    att_recv(2, 0, 2)
     go.second_last(0)
+    att_recv(2, 2, 4)
     go.second_recv(3)
     att_recv(2, 4, 8)
     go.second_last(1)
     go.second_last(2)
-    att_recv(3, 0, 4)
+    att_recv(3, 0, 2)
     go.second_last(3)
-    att_recv(3, 4, 8)
+    att_recv(3, 2, 8)
     go.finish()
-    hand_out(early)
     for k in (0, -1, 1, -2, 2, -3, 3):
         out_step(z + k)
+    hand_out(early)
     att_recv(4, 0, 4)
     out_step(z + 4)
+
 
     col = jnp.zeros((TOK, 1), F32)
     for sx in range(4):
@@ -518,22 +524,22 @@
             out = out + jnp.dot(HB[sx], WO[head * 4 + sx, :, 512:768], preferred_element_type=F32)
         PP[dest] = out
 
-    rs_sent = []
+    def rs_at(way, part, s):
+        d = 0 if way > 0 else 14
+        long = Ring.LONG[way]
+        return d + (4 * long.index(part) + s if part in long else 8 + 3 * Ring.LONG[-way].index(part) + s)
 
     def rs_copy(way, part, s):
-        d = 0 if way > 0 else 1
-        return rcopy(RSS.at[d, part, s], RSR.at[d, part, s], rss.at[d, part, s],
-                     rsr.at[d, part, s], device(x, y, z + way, c))
+        n = rs_at(way, part, s)
+        return rcopy(RSS.at[n], RSR.at[n], rss, rsr.at[n], device(x, y, z + way, c))
 
     def rs_send(way, part, s, value):
-        RSS[0 if way > 0 else 1, part, s] = value.astype(BF)
-        cp = rs_copy(way, part, s)
-        cp.start()
-        rs_sent.append(cp)
+        RSS[rs_at(way, part, s)] = value.astype(BF)
+        rs_copy(way, part, s).start()
 
     def rs_recv(way, part, s):
         rs_copy(way, part, s).wait_recv()
-        return RSR[0 if way > 0 else 1, part, s].astype(F32)
+        return RSR[rs_at(way, part, s)].astype(F32)
 
     def hops(way, part):
         return 4 if part in Ring.LONG[way] else 3
@@ -552,11 +558,8 @@
     eye = (lax.broadcasted_iota(jnp.int32, (TOK, TOK), 0)
            == lax.broadcasted_iota(jnp.int32, (TOK, TOK), 1))
     SS[z] = jnp.sum(jnp.where(eye, col, 0.0), axis=0, keepdims=True)
-    ss_sent = []
     for k in range(1, 8):
-        cp = rcopy(SS.at[z], SS.at[z], sss.at[k], ssr.at[k], device(x, y, z + k, c))
-        cp.start()
-        ss_sent.append(cp)
+        rcopy(SS.at[z], SS.at[z], sss, ssr, device(x, y, z + k, c)).start()
     for k in (2, -2, 1, -1, 0):
         partial(z + k)
     ring_order = ((1, 0), (-1, 2), (1, 1), (-1, 3), (1, 2), (-1, 0), (1, 3), (-1, 1))
@@ -564,11 +567,10 @@
         for way, part in ring_order:
             if s < hops(way, part) - 1:
                 rs_send(way, part, s + 1, rs_recv(way, part, s) + own_part(way, part, s + 1))
-    ss_total = SS[z]
+    rcopy(SS.at[pl.ds(0, 7)], SS.at[pl.ds(0, 7)], sss, ssr, sib).wait_recv()
+    ss_total = SS[0]
     for k in range(1, 8):
-        origin = lax.rem(z - k + 16, 8)
-        rcopy(SS.at[origin], SS.at[origin], sss.at[k], ssr.at[k], device(x, y, z + k, c)).wait_recv()
-        ss_total = ss_total + SS[origin]
+        ss_total = ss_total + SS[k]
     r1 = lax.rsqrt(jnp.sum(jnp.where(eye, ss_total, 0.0), axis=1, keepdims=True) / 5120.0 + EPS)
 
     for part in range(4):
@@ -580,37 +582,31 @@
         VAL[rows, 384:512] = kv[:, 128:256].astype(BF)
 
     SEND1[:, :, 0:256] = head_rows(slice(256, 512)).astype(BF).reshape(32, 16, 256)
-    tail = tail + tail_rows(2) + tail_rows(3)
+    tail = tails[0] + tail_rows(2) + tail_rows(3)
     SEND1[:, :, 256:384] = tail.astype(BF).reshape(32, 16, 128)
     hand_out(late)
 
-    def landed(srcs, dsts):
-        def step(d, carry):
-            for (src, _, ss, rs), dst in zip(srcs(d), dsts):
-                rcopy(src, dst.at[d], ss.at[d], rs.at[d], target(d)).wait_recv()
-
-            @pl.when(jnp.logical_not(same(d)))
-            def _():
-                for (src, _, ss, rs), dst in zip(srcs(d), dsts):
-                    rcopy(src, dst.at[d], ss.at[d], rs.at[d], target(d)).wait_send()
-            return carry
-
-        lax.fori_loop(0, 32, step, 0)
+    def landed(groups):
+        for dst, ss, rs in groups:
+            rcopy(dst, dst, ss, rs, sib).wait_recv()
+
+            @pl.when(a == c)
+            def _(dst=dst, ss=ss, rs=rs):
+                most = dst.at[pl.ds(0, 31)]
+                rcopy(most, most, ss, rs, sib).wait_send()
+
+            @pl.when(a != c)
+            def _(dst=dst, ss=ss, rs=rs):
+                rcopy(dst, dst, ss, rs, sib).wait_send()
 
     for part in (ring, gq, go, att):
         part.drain()
-    for cp in ss_sent + rs_sent:
-        cp.wait_send()
-    for u in range(2):
-        shift(u).wait_send()
-    gq.first_drain()
-    for ol in range(4):
-        for part in range(4):
-            rows = pl.ds(80 * part, 80)
-            rcopy(XX.at[8 + ol, rows], XX.at[2 * ol + c, rows],
-                  xcs.at[ol, part], xcr.at[ol, part], sib).wait_send()
-
-    landed(early, (info_land, land0))
+    rcopy(RSS, RSS, rss, rsr.at[0], sib).wait_send()
+    rcopy(SS.at[pl.ds(0, 7)], SS.at[pl.ds(0, 7)], sss, ssr, sib).wait_send()
+    rcopy(WOS, WOS, ts, tr.at[0], sib).wait_send()
+    rcopy(XX.at[pl.ds(0, 4)], XX.at[pl.ds(0, 4)], xcs, xcr.at[0], sib).wait_send()
+
+    landed(((info_land, ns, nr), (land0, es, er)))
     lane = lax.broadcasted_iota(jnp.int32, (32, 128), 1)
     hit = jnp.logical_and(info_land[...].reshape(32, 128) == e, lane < 16)
     here = jnp.max(hit.astype(F32), axis=1, keepdims=True)
@@ -631,7 +627,7 @@
     rows0 = settle(land0[...].reshape(512, 256))
     for f in range(2):
         OUT[f, 0:16] = rows0[:, :, 128 * f:128 * f + 128]
-    landed(late, (land1,))
+    landed(((land1, fs, fr),))
     rows1 = settle(land1[...].reshape(512, 384))
     for f in range(2):
         OUT[2 + f, 0:16] = rows1[:, :, 128 * f:128 * f + 128]
@@ -681,15 +677,14 @@
             vmem((12, TOK, 640), BF), vmem((32, 160, WC), BF), vmem((32, 160, WC), BF),
             vmem((8, TOK, 512), BF), vmem((TOK, WC), F32),
             vmem((4, TOK, 160), F32), vmem((4, TOK, 160), BF), vmem((8, TOK, 256), F32),
-            vmem((2, 4, 4, 80, 256), BF), vmem((2, 4, 4, 80, 256), BF), vmem((8, 1, TOK), F32),
+            vmem((28, 80, 256), BF), vmem((28, 80, 256), BF), vmem((8, 1, TOK), F32),
             vmem((32, 16, 256), BF), vmem((32, 16, 384), BF), vmem((TOK, 512), BF),
             vmem((1, 128), jnp.int32), vmem((1, 128), jnp.int32),
             dma((12,)), dma((3,)), dma, dma((2,)), dma((2,)),
-            dma((2, 4, 4)), dma((2, 4, 4)), dma((4, 4)), dma((4, 4)),
-            dma((2, 36)), dma((2, 36)), dma((2,)), dma((2,)), dma((2, 36)), dma((2, 36)),
-            dma((2, 4, 4)), dma((2, 4, 4)), dma((2, 4, 4)), dma((2, 4, 4)),
-            dma((8,)), dma((8,)), dma((32,)), dma((32,)), dma((32,)), dma((32,)),
-            dma((32,)), dma((32,)),
+            dma, dma((2, 4, 4)), dma, dma((4,)),
+            dma, dma((2, 20)), dma, dma, dma((2,)), dma, dma((2, 20)), dma,
+            dma, dma((2, 4, 4)), dma, dma((28,)),
+            dma, dma, dma, dma, dma, dma, dma, dma,
         ],
         compiler_params=pltpu.CompilerParams(
             collective_id=0, has_side_effects=True, vmem_limit_bytes=58 * 2**20),

time: 135 us -> 126 us (0.933)
  Pallas kernels: 131 us -> 123 us
    pallas_call x1, Pallas kernels: 131 us -> 123 us  [body(): pl.pallas_call(mega, out_shape=jax.ShapeDtypeStruct((4, SPAN, 32, 128), B...]
where the time goes in v3:
time: 126 us; the launch traced here: 125 us
  Pallas kernels  123 us (98%)
  local copies, waits for them, and re-layouts  1.98 us (2%)
    pallas_call x1, Pallas kernels, body(): pl.pallas_call(mega, out_shape=jax.ShapeDtypeStruct((4, SPAN, 32, 128), B...  123 us

profile of v3, /device:TPU:39, one launch (start us, length us, event | category | flops | bytes accessed | tf_op | source)
XLA Modules:
  0.0 124.5 jit_solution(2610068973521954434)
XLA Ops:
  0.0 122.5 %prefill.1 = bf16[4,20,32,128]{3,2,1,0:T(8,128)(2,1)} custom-call(bf16[320,640]{1,0:T(8,128)(2,1)} %bitcast.10, bf16[160,512]{1,0:T(8,128)(2,1)} %q_in.1, bf16[160,2,128]{2,1,0:T(2,128)(2,1)} %kv0_in.1, bf16[160,512]{1,0:T(8,128)(2,1)} %out_in.1, bf16[160,2,128]{2,1,0:T(2,128)(2,1)} %kv1_in.1, s32[1,16]{1,0:T(1,128)} %bitcast.11, s32[1,16]{1,0:T(1,128)} %bitcast.12, ...), custom_call_target="tpu_custom_call" | custom-call | tf_op jit(solution)/shard_map/prefill/pallas_call | solution.py:664
  122.5 2.0 %copy.16 = bf16[2,2,32,20,128]{4,2,3,1,0:T(8,128)(2,1)} copy(bf16[2,2,32,20,128]{4,2,3,1,0:T(8,128)(2,1)} %bitcast.9) | data formatting | bytes 1310720

commit v4 on v3

--- a/solution.py
+++ b/solution.py
@@ -186,7 +186,7 @@
 def mega(tok_in, q_in, kv0_in, out_in, kv1_in, dest_in, len_in, gains_in, qg_in, kg_in,
          cos_in, sin_in, mask_in, lanes_in, caches,
          XS, KV0, KV1, DEST, LEN, gains, qg, kg, cos, sin, mask, lanes, land0, land1, info_land, OUT,
-         WQS, WOS, XX, WQ, WO, A, ACC, HID, HB, PP, RSS, RSR, SS, SEND0, SEND1, VAL, INFO, MY,
+         WQS, WOS, XX, WQ, WO, A, ACC, HID, HB, PP, RSS, RSR, SS, SEND0, SEND1, VAL, INFO, MY, XN,
          in_sem, own_sem, out_sem, swap_s, swap_r, xs, xr, xcs, xcr, wqs, wqr, wqc, ts, tr, wos, wor, woc,
          as_, ar, rss, rsr, sss, ssr, es, er, fs, fr, ns, nr):
     e = lax.axis_index("engine")
@@ -353,34 +353,36 @@
     gq.second_last(3)
     shift_recv()
     go.first()
-    gq.finish()
     own_x.wait()
     for n in range(5, 12):
         fetch[n].wait()
 
+    def scale_step(i, total):
+        xv = XX[i].astype(F32)
+        gain = gains[0:1, pl.ds(pl.multiple_of(640 * i, 128), 640)]
+        XN[i] = (xv * gain).astype(BF)
+        return total + jnp.sum(xv * xv, axis=1, keepdims=True)
+
+    def qkv_step(i, carry):
+        w = WQ[pl.ds(4 * i, 4)].reshape(640, WC)
+        ACC[...] += jnp.dot(XN[i], w, preferred_element_type=F32)
+        return carry
+
+    def chunk(j):
+        return 2 * lax.rem(zl + 1 + j // 2, 4) + lax.rem(j, 2)
+
     ACC[...] = jnp.zeros_like(ACC)
-
-    def qkv_step(i, total):
-        xv = XX[i].astype(F32)
-        total = total + jnp.sum(xv * xv, axis=1, keepdims=True)
-        xn = (xv * gains[0:1, pl.ds(pl.multiple_of(640 * i, 128), 640)]).astype(BF)
-        w = WQ[pl.ds(4 * i, 4)].reshape(640, WC)
-        ACC[...] += jnp.dot(xn, w, preferred_element_type=F32)
-        return total
-
     for n in range(1, 4):
         x_crossed(lax.rem(zl + n, 4))
-    total = jnp.zeros((TOK, 1), F32)
-
-    def some(low, high, total):
-        return lax.fori_loop(
-            low, high, lambda j, s: qkv_step(2 * lax.rem(zl + 1 + j // 2, 4) + lax.rem(j, 2), s), total)
-
-    total = some(0, 6, total)
+    total = lax.fori_loop(0, 6, lambda j, s: scale_step(chunk(j), s), jnp.zeros((TOK, 1), F32))
     x_recv(4, 0, 4)
+    gq.finish()
+    lax.fori_loop(0, 3, lambda j, s: qkv_step(chunk(j), s), 0)
     go.first_recv()
+    lax.fori_loop(3, 6, lambda j, s: qkv_step(chunk(j), s), 0)
     x_crossed(zl)
-    total = some(6, 8, total)
+    total = lax.fori_loop(6, 8, lambda j, s: scale_step(chunk(j), s), total)
+    lax.fori_loop(6, 8, lambda j, s: qkv_step(chunk(j), s), 0)
     r0 = lax.rsqrt(total / 5120.0 + EPS)
     cosv, sinv = cos[...], sin[...]
     VAL[:, 0:128] = rope(head_norm(ACC[:, 512:640] * r0, kg[0:1]), cosv, sinv).astype(BF)
@@ -679,7 +681,7 @@
             vmem((4, TOK, 160), F32), vmem((4, TOK, 160), BF), vmem((8, TOK, 256), F32),
             vmem((28, 80, 256), BF), vmem((28, 80, 256), BF), vmem((8, 1, TOK), F32),
             vmem((32, 16, 256), BF), vmem((32, 16, 384), BF), vmem((TOK, 512), BF),
-            vmem((1, 128), jnp.int32), vmem((1, 128), jnp.int32),
+            vmem((1, 128), jnp.int32), vmem((1, 128), jnp.int32), vmem((8, TOK, 640), BF),
             dma((12,)), dma((3,)), dma, dma((2,)), dma((2,)),
             dma, dma((2, 4, 4)), dma, dma((4,)),
             dma, dma((2, 20)), dma, dma, dma((2,)), dma, dma((2, 20)), dma,

time: 126 us -> 125 us (level)
  no operation moved by 1% of the time
where the time goes in v4:
time: 125 us; the launch traced here: 124 us
  Pallas kernels  122 us (98%)
  local copies, waits for them, and re-layouts  1.98 us (2%)
    pallas_call x1, Pallas kernels, body(): pl.pallas_call(mega, out_shape=jax.ShapeDtypeStruct((4, SPAN, 32, 128), B...  122 us

profile of v4, /device:TPU:39, one launch (start us, length us, event | category | flops | bytes accessed | tf_op | source)
XLA Modules:
  0.0 124.0 jit_solution(10076586003452118410)
XLA Ops:
  0.0 122.0 %prefill.1 = bf16[4,20,32,128]{3,2,1,0:T(8,128)(2,1)} custom-call(bf16[320,640]{1,0:T(8,128)(2,1)} %bitcast.10, bf16[160,512]{1,0:T(8,128)(2,1)} %q_in.1, bf16[160,2,128]{2,1,0:T(2,128)(2,1)} %kv0_in.1, bf16[160,512]{1,0:T(8,128)(2,1)} %out_in.1, bf16[160,2,128]{2,1,0:T(2,128)(2,1)} %kv1_in.1, s32[1,16]{1,0:T(1,128)} %bitcast.11, s32[1,16]{1,0:T(1,128)} %bitcast.12, ...), custom_call_target="tpu_custom_call" | custom-call | tf_op jit(solution)/shard_map/prefill/pallas_call | solution.py:666
  122.0 2.0 %copy.16 = bf16[2,2,32,20,128]{4,2,3,1,0:T(8,128)(2,1)} copy(bf16[2,2,32,20,128]{4,2,3,1,0:T(8,128)(2,1)} %bitcast.9) | data formatting | bytes 1310720
